TPU v7x, 256 devices: a whole 4x4x8 slice. The times are simulated.
256 devices in a mesh: coil: 8 (over x, core), slab: 32 (over z, y).
Axes of the slice: x: 4, y: 4, z: 8, core: 2. Of those that a mesh axis runs over, the one named last changes fastest.
Arguments:
- cotangent: float32 [2, 8, 256, 256], P(None, None, 'slab'), may hold values from -40 to 40
- sensitivity: float32 [8, 2, 8, 256, 256], P('coil', None, None, 'slab'), may hold values from -1.5 to 1.5
- kernel: float32 [512, 16, 512], P('slab'), may hold values from 0.2 to 2
- reg_weight: float32 [1], replicated, may hold values from 0.2 to 2
Outputs:
- solution: float32 [2, 8, 256, 256], P(None, None, 'slab')
All inputs are finite; a program needn't handle non-finite values.
Results may differ from a plain program's by a relative error of at most 0.0001.
Values sent between devices are 32-bit elements; how exact they have to be, the bound alone decides.
No kernel may reach another device: no remote copies, remote signals or barrier semaphores. Data moves between devices by JAX's collectives and lax.ppermute only.
A program may use at most 64 MiB of HBM per device.

v0:
```python
from functools import partial
import math

import jax
import jax.numpy as jnp
import numpy as np
from jax import lax
from jax.experimental import pallas as pl
from jax.experimental.pallas import tpu as pltpu
from jax.sharding import PartitionSpec as P

F32 = jnp.float32
BF16 = jnp.bfloat16
NN = ((1,), (0,))
NT = ((1,), (1,))


def dft(length):
    grid_size = 2 * length
    winding = np.outer(np.arange(length) + length // 2, np.arange(grid_size)) % grid_size
    return np.exp(-2j * np.pi * winding / grid_size) / math.sqrt(grid_size)


def halves(table, axis):
    high = table.astype(np.float32).astype(jnp.bfloat16)
    low = (table - high.astype(np.float64)).astype(np.float32).astype(jnp.bfloat16)
    return jnp.asarray(np.concatenate([high, low], axis=axis))


def pair_of(ref, axis):
    half = ref.shape[axis] // 2
    return (ref[:half], ref[half:]) if axis == 0 else (ref[:, :half], ref[:, half:])


def plane_table(length):
    table = dft(length)
    return np.concatenate([table.real, table.imag], axis=1)


def rows_table(length, slabs, scale):
    pairs = length // slabs // 2
    table = scale * dft(length)[:, :length].reshape(slabs, pairs, 2, length).transpose(2, 0, 1, 3)
    out = np.empty((2, slabs, 2, pairs, 2, length))
    out[:, :, 0, :, 0], out[:, :, 1, :, 0] = table.real, -table.imag
    out[:, :, 0, :, 1], out[:, :, 1, :, 1] = table.imag, table.real
    return out.reshape(2 * length, 2 * length)


def split(values):
    high = values.astype(BF16)
    low = (values - high.astype(F32)).astype(BF16)
    return high, low


def product(left, right, dims):
    dot = partial(lax.dot_general, dimension_numbers=(dims, ((), ())), preferred_element_type=F32)
    rows, cols = left[0].shape[0], right[0].shape[1 - dims[1][0]]
    if dims == NT and cols <= 128:
        both = dot(left[0], jnp.concatenate(right, axis=0))
        return (both[:, :cols] + both[:, cols:]) + dot(left[1], right[0])
    both = dot(jnp.concatenate(left, axis=0), right[0])
    return (both[:rows] + both[rows:]) + dot(left[0], right[1])


def exchange(tiles):
    count = len(tiles)
    width = tiles[0].shape[1]
    step = width // count
    group = lax.broadcasted_iota(jnp.int32, tiles[0].shape, 1) // step
    tiles = [pltpu.roll(tile, step * at, 1) if at else tile for at, tile in enumerate(tiles)]
    half = 1
    while half < count:
        later = (group // half) % 2 == 1
        tiles = [jnp.where(later, tiles[(at + half) % count], tiles[at]) for at in range(count)]
        half *= 2
    return [pltpu.roll(tiles[-at], width - step * at, 1) if at else tiles[0] for at in range(count)]


def coil_product(sens_ref, real, imag):
    rows = real.shape[0]
    sens_re, sens_im = sens_ref[:rows], sens_ref[rows:]
    return sens_re * real - sens_im * imag, sens_re * imag + sens_im * real


def send_columns(real, imag, table, out_ref, straight_ref, turned_ref):
    cells, width = real.shape
    rows, grid_size = 8, 2 * width
    planes, blocks = cells // rows, grid_size // 128
    for plane in range(planes):
        for lanes in range(0, width, 128):
            at = 2 * rows * plane + lanes // 128 * 2 * cells
            one = real[rows * plane : rows * (plane + 1), lanes : lanes + 128]
            other = imag[rows * plane : rows * (plane + 1), lanes : lanes + 128]
            straight_ref[at : at + rows], straight_ref[at + rows : at + 2 * rows] = one, other
            turned_ref[at : at + rows], turned_ref[at + rows : at + 2 * rows] = -other, one

    def by_parity(ref):
        parts = [
            jnp.concatenate(
                [ref[pl.ds(lanes * 2 * cells + parity, cells, stride=2), :] for lanes in range(width // 128)], axis=1
            )
            for parity in range(2)
        ]
        return split(jnp.concatenate(parts, axis=0))

    straight, turned = by_parity(straight_ref), by_parity(turned_ref)
    high, low = table()
    spec = product(straight, (high[:, :grid_size], low[:, :grid_size]), NN)
    spec = spec + product(turned, (high[:, grid_size:], low[:, grid_size:]), NN)
    tiles = [
        jnp.concatenate(
            [
                spec[(parity * planes + plane) * rows :][:rows, block * 128 : (block + 1) * 128]
                for parity in range(2)
                for block in range(blocks)
            ],
            axis=0,
        )
        for plane in range(planes)
    ]
    tiles = exchange(tiles)
    for parity in range(2):
        for block in range(blocks):
            for at in range(planes):
                start = (parity * blocks + block) * rows
                out_ref[block * planes + at, parity * rows : (parity + 1) * rows, :] = tiles[at][
                    start : start + rows
                ]


def turn(value, power):
    real, imag = value
    power %= 16
    if power == 0:
        return real, imag
    if power == 4:
        return imag, -real
    if power == 8:
        return -real, -imag
    if power == 12:
        return -imag, real
    cos, sin = math.cos(math.pi * power / 8), -math.sin(math.pi * power / 8)
    return cos * real - sin * imag, cos * imag + sin * real


def plus(one, other):
    return one[0] + other[0], one[1] + other[1]


def minus(one, other):
    return one[0] - other[0], one[1] - other[1]


def four(values, power):
    even, even_off = plus(values[0], values[2]), minus(values[0], values[2])
    odd, odd_off = plus(values[1], values[3]), turn(minus(values[1], values[3]), power)
    return plus(even, odd), plus(even_off, odd_off), minus(even, odd), minus(even_off, odd_off)


def deepen(cells):
    out = [None] * 16
    for rest in range(4):
        folded = [plus(cells[at], turn(cells[at + 4], 4 * rest)) for at in range(4)]
        folded = [turn(value, (at + 4) * rest) for at, value in enumerate(folded)]
        for at, value in enumerate(four(folded, 4)):
            out[4 * at + rest] = value
    return out


def shallow(freqs):
    out = [None] * 8
    for rest in range(4):
        folded = four([freqs[4 * at + rest] for at in range(4)], -4)
        for at in range(4):
            value = turn(folded[at], -(at + 4) * rest)
            above = turn(value, -4 * rest)
            out[at] = value if rest == 0 else plus(out[at], value)
            out[at + 4] = above if rest == 0 else plus(out[at + 4], above)
    return out


def spectrum(in_ref, rows_ref):
    slabs, _, lanes = in_ref.shape
    high, low = pair_of(rows_ref, 0)
    length = high.shape[0] // 2
    parity = []
    for at in range(2):
        cells = in_ref[:, at * 8 : (at + 1) * 8, :].reshape(slabs * 8, lanes).T
        rows = slice(at * length, (at + 1) * length)
        parity.append(product(split(cells), (high[rows], low[rows]), NN))
    total_of, differ = parity[0] + parity[1], parity[0] - parity[1]
    real = jnp.concatenate([total_of[:, :length], differ[:, :length]], axis=1)
    imag = jnp.concatenate([total_of[:, length:], differ[:, length:]], axis=1)
    cols = lanes // 8
    return deepen([(real[at * cols : (at + 1) * cols], imag[at * cols : (at + 1) * cols]) for at in range(8)])


def at_depth(ref, at):
    cols = 16
    tiles = [
        ref[pl.ds(tile * 16 * cols + at, cols, stride=16), :] for tile in range(ref.shape[0] // (16 * cols))
    ]
    return jnp.concatenate(tiles, axis=1)


def total(values):
    return jnp.sum(jnp.sum(values, axis=0, keepdims=True), axis=1, keepdims=True)


def along(part, whole):
    return jnp.where(whole > 0.0, part / jnp.where(whole > 0.0, whole, 1.0), 0.0)


def row_of(value, lanes):
    return jnp.broadcast_to(value, (1, lanes))


def start_kernel(*refs):
    count = (len(refs) - 4) // 2
    sources, out_ref, loaded = refs[:count], refs[count], refs[count + 1 : 2 * count + 1]
    sems, *spaces = refs[2 * count + 1 :]
    pairs = []
    for source, target in zip(sources, loaded):
        rows, lanes = source.shape[0], target.shape[1]
        for tile in range(source.shape[1] // lanes):
            pairs.append((source.at[:, pl.ds(tile * lanes, lanes)], target.at[pl.ds(tile * rows, rows)]))
    copies = [pltpu.make_async_copy(*pair, sems.at[at]) for at, pair in enumerate(pairs)]
    for copy in copies:
        copy.start()
    for copy in copies[:2]:
        copy.wait()
    vec_ref, sens_ref, table_ref = loaded[:3]
    cells = vec_ref.shape[0] // 2
    real, imag = coil_product(sens_ref, vec_ref[:cells], vec_ref[cells:])

    def table():
        copies[2].wait()
        return pair_of(table_ref, 0)

    send_columns(real, imag, table, out_ref, *spaces)
    for copy in copies[3:]:
        copy.wait()


def filter_kernel(in_ref, kernel_ref, rows_ref, out_ref, spec_ref, energy_ref, by_depth_ref):
    slabs, _, lanes = in_ref.shape
    spec = spectrum(in_ref, rows_ref)
    cols = lanes // 8
    weight = 0.0
    filtered = []
    for at, (real, imag) in enumerate(spec):
        spec_ref[2 * at * cols : (2 * at + 1) * cols] = real
        spec_ref[(2 * at + 1) * cols : (2 * at + 2) * cols] = imag
        kernel = at_depth(kernel_ref, at)
        by_depth_ref[at * cols : (at + 1) * cols] = kernel
        filtered.append((kernel * real, kernel * imag))
        weight = weight + (filtered[-1][0] * real + filtered[-1][1] * imag)
    energy_ref[...] = jnp.broadcast_to(total(weight), energy_ref.shape)
    planes = shallow(filtered)
    real, imag = [jnp.concatenate([plane[part] for plane in planes], axis=0) for part in range(2)]
    high, low = pair_of(rows_ref, 0)
    length = high.shape[0] // 2
    for at, join in enumerate((jnp.add, jnp.subtract)):
        folded = [join(part[:, :length], part[:, length:]) for part in (real, imag)]
        rows = slice(at * length, (at + 1) * length)
        back = product((high[rows], low[rows]), split(jnp.concatenate(folded, axis=1)), NT)
        out_ref[:, at * 8 : (at + 1) * 8, :] = back.reshape(slabs, 8, lanes)


def image_kernel(in_ref, sens_ref, table_ref, out_ref, straight_ref, turned_ref):
    slabs, _, lanes = in_ref.shape
    planes, blocks = 8, slabs // 8
    tiles = [
        jnp.concatenate(
            [
                in_ref[block * planes + at, part * 8 : (part + 1) * 8, :]
                for part in range(2)
                for block in range(blocks)
            ],
            axis=0,
        )
        for at in range(planes)
    ]
    tiles = exchange(tiles)
    spec = jnp.concatenate(
        [
            jnp.concatenate(
                [
                    tiles[plane][(part * blocks + block) * 8 : (part * blocks + block + 1) * 8]
                    for block in range(blocks)
                ],
                axis=1,
            )
            for part in range(2)
            for plane in range(planes)
        ],
        axis=0,
    )
    spec = split(spec)
    grid_size = blocks * 128
    high, low = pair_of(table_ref, 0)
    by_real = product(spec, (high[:, :grid_size], low[:, :grid_size]), NT)
    by_imag = product(spec, (high[:, grid_size:], low[:, grid_size:]), NT)
    cells = planes * 8
    tiled = range(by_real.shape[1] // 128)
    for parity in range(2):
        part = slice(parity * cells, (parity + 1) * cells)
        for tile in tiled:
            rows, tile_of = pl.ds(tile * 2 * cells + parity, cells, stride=2), slice(tile * 128, tile * 128 + 128)
            straight_ref[rows, :] = by_real[part, tile_of]
            turned_ref[rows, :] = by_imag[part, tile_of]

    def of_part(ref, part):
        columns = []
        for tile in tiled:
            starts = [tile * 2 * cells + 16 * plane + 8 * part for plane in range(planes)]
            columns.append(jnp.concatenate([ref[start : start + 8] for start in starts], axis=0))
        return jnp.concatenate(columns, axis=1)

    img_re = of_part(straight_ref, 0) + of_part(turned_ref, 1)
    img_im = of_part(straight_ref, 1) - of_part(turned_ref, 0)
    sens_re, sens_im = sens_ref[:cells], sens_ref[cells:]
    out_ref[:cells] = sens_re * img_re + sens_im * img_im
    out_ref[cells:] = sens_re * img_im - sens_im * img_re


def add_kernel(own_ref, next_ref, across_ref, last_ref, out_ref):
    out_ref[...] = (own_ref[...] + across_ref[...]) + (next_ref[...] + last_ref[...])


def turn_kernel(
    lam_ref, one_ref, other_ref, vec_ref, sens_ref, table_ref, out_ref, image_ref, sums_ref, straight_ref, turned_ref
):
    cells2, width = vec_ref.shape
    cells = cells2 // 2
    vec = vec_ref[...]
    image = (one_ref[...] + other_ref[...]) + lam_ref[0] * vec
    image_ref[...] = image
    real, imag = coil_product(sens_ref, image[:cells], image[cells:])
    send_columns(real, imag, partial(pair_of, table_ref, 0), out_ref, straight_ref, turned_ref)
    norm = total(vec * vec)
    ratio = along(total(vec * image), norm)
    rest = image - ratio * vec
    row = lax.broadcasted_iota(jnp.int32, sums_ref.shape, 0)
    lanes = sums_ref.shape[1]
    sums_ref[...] = jnp.where(
        row == 0,
        row_of(norm, lanes),
        jnp.where(row == 1, row_of(ratio, lanes), row_of(total(rest * rest), lanes)),
    )


def last_kernel(in_ref, before_ref, energy_ref, sums_ref, by_depth_ref, rows_ref, out_ref):
    spec = spectrum(in_ref, rows_ref)
    cols = spec[0][0].shape[0]
    norm = energy_ref[0:1, 0:1]

    def before(at):
        return before_ref[2 * at * cols : (2 * at + 1) * cols], before_ref[(2 * at + 1) * cols : (2 * at + 2) * cols]

    def kernel(at):
        return by_depth_ref[at * cols : (at + 1) * cols]

    weight = 0.0
    for at, (real, imag) in enumerate(spec):
        real_0, imag_0 = before(at)
        weight = weight + kernel(at) * (real * real_0 + imag * imag_0)
    ratio = along(total(weight), norm)
    weight = 0.0
    for at, (real, imag) in enumerate(spec):
        real_0, imag_0 = before(at)
        real, imag = real - ratio * real_0, imag - ratio * imag_0
        weight = weight + kernel(at) * (real * real + imag * imag)
    lanes = out_ref.shape[1]
    values = [
        row_of(norm, lanes),
        row_of(ratio, lanes),
        row_of(total(weight), lanes),
        sums_ref[0:1],
        sums_ref[1:2],
        sums_ref[2:3],
    ]
    lane = lax.broadcasted_iota(jnp.int32, (1, lanes), 1)
    line = values[-1]
    for at, value in enumerate(values[:-1]):
        line = jnp.where(lane == at, value, line)
    out_ref[...] = jnp.broadcast_to(line, out_ref.shape)


def solution_kernel(lam_ref, all_ref, vec_ref, image_ref, out_ref):
    lam = lam_ref[0]
    every = all_ref[...]
    lane = lax.broadcasted_iota(jnp.int32, every.shape, 1)

    def column(at):
        return jnp.sum(jnp.where(lane == at, every, 0.0), axis=1, keepdims=True)

    def sum_of(values):
        return jnp.sum(values, axis=0, keepdims=True)

    deep_norm, deep_ratio, deep_rest, norms, ratios, rests = [column(at) for at in range(6)]
    norm = sum_of(norms) * 0.125
    curvature = sum_of(ratios * norms) * 0.125
    step = norm / curvature
    left, deep_left = 1.0 - step * ratios, 1.0 - step * deep_ratio
    fresh = sum_of(left * left * norms + step * step * rests) * 0.125
    cross = sum_of(ratios * norms * left - step * rests) * 0.125
    energy_now = sum_of(deep_left * deep_left * deep_norm + step * step * deep_rest)
    ratio = fresh / norm
    bent = energy_now + lam * fresh + ratio * (2.0 * cross + ratio * curvature)
    step_now = along(fresh, bent)
    vec = vec_ref[...]
    residual = vec - step * image_ref[...]
    out_ref[...] = step * vec + step_now * (residual + ratio * vec)


def call(kernel, shapes, places, scratch=(), limit=16):
    spaces = {"s": pltpu.SMEM, "v": pltpu.VMEM, "h": pltpu.HBM}
    outs = [jax.ShapeDtypeStruct(shape, F32) if isinstance(shape, tuple) else shape for shape in shapes]
    out_specs = [pl.BlockSpec(memory_space=pltpu.VMEM)] * len(shapes)
    return pl.pallas_call(
        kernel,
        out_shape=outs if len(outs) > 1 else outs[0],
        in_specs=[pl.BlockSpec(memory_space=spaces[place]) for place in places],
        out_specs=out_specs if len(outs) > 1 else out_specs[0],
        scratch_shapes=list(scratch),
        compiler_params=pltpu.CompilerParams(vmem_limit_bytes=limit * 2**20),
    )


def shards(cotangent, sensitivity, kernel, reg_weight):
    planes, rows, width = cotangent.shape[1:]
    slabs = lax.axis_size("slab")
    coils = lax.axis_size("coil")
    cols = kernel.shape[0]
    cells2 = 2 * planes * rows
    vec = cotangent.reshape(cells2, width)
    sens = sensitivity.reshape(cells2, width)
    filt = kernel.reshape(cols * kernel.shape[1], kernel.shape[2])
    table = halves(plane_table(width), 0)
    row_table = halves(rows_table(width, slabs, 1.0 / math.sqrt(2 * planes)), 0)
    lanes = planes * cols
    block = (slabs, 2 * rows, lanes)
    to_slabs = partial(lax.all_to_all, axis_name="slab", split_axis=0, concat_axis=0, tiled=True)
    dma = pltpu.SemaphoreType.DMA

    spaces = [pltpu.VMEM((cells2 * width // 128, 128), F32)] * 2
    sources = [pltpu.with_memory_space_constraint(array, pltpu.HBM) for array in (vec, sens, table, filt, row_table)]
    loaded = [pltpu.VMEM(array.shape, array.dtype) for array in sources]
    loaded[3] = pltpu.VMEM((filt.size // 128, 128), F32)
    sent, vec, sens, table, filt, row_table = call(
        start_kernel, [block, *loaded], "hhhhh", [dma((len(sources) + filt.shape[1] // 128 - 1,)), *spaces]
    )(*sources)
    got = to_slabs(sent)
    shapes = [block, (4 * lanes, 2 * width), (8, 128), (2 * lanes, 2 * width)]
    back, before, energy_now, filt = call(filter_kernel, shapes, "vvv", (), 32)(got, filt, row_table)
    home = to_slabs(back)
    term = call(image_kernel, [(cells2, width)], "vvv", spaces)(home, sens, table)

    chips = coils // 2

    def from_chip(shift):
        pairs = [
            (2 * chip + core, 2 * ((chip + shift) % chips) + core) for chip in range(chips) for core in range(2)
        ]
        return lax.ppermute(term, "coil", pairs)

    across = from_chip(2)
    pair = call(add_kernel, [term.shape], "vvvv")(term, from_chip(1), across, from_chip(3))
    other = lax.ppermute(pair, "coil", [(at, at ^ 1) for at in range(coils)])
    sent, image, sums = call(turn_kernel, [block, (cells2, width), (8, 128)], "svvvvv", spaces)(
        reg_weight, pair, other, vec, sens, table
    )
    got = to_slabs(sent)
    own = call(last_kernel, [(coils * slabs, 128)], "vvvvvv", (), 32)(
        got, before, energy_now, sums, filt, row_table
    )
    every = lax.all_to_all(own, ("coil", "slab"), 0, 0, tiled=True)
    result = call(solution_kernel, [(cells2, width)], "svvv")(reg_weight, every, vec, image)
    return result.reshape(cotangent.shape)


def solution(mesh):
    in_specs = (
        P(None, None, "slab", None),
        P("coil", None, None, "slab", None),
        P("slab", None, None),
        P(),
    )
    out_specs = P(None, None, "slab", None)
    return jax.shard_map(shards, mesh=mesh, in_specs=in_specs, out_specs=out_specs, check_vma=False)
```

profile of v0, /device:TPU:1, one launch (start us, length us, event | category | flops | bytes accessed | tf_op | source)
XLA Modules:
  0.0 94.6 jit_solution(17514165046068764266)
XLA Ops:
  0.0 2.0 %shard_map.64 = (f32[32,16,128]{2,1,0:T(8,128)S(1)}, f32[128,256]{1,0:T(8,128)S(1)}, f32[128,256]{1,0:T(8,128)S(1)}, bf16[512,1024]{1,0:T(8,128)(2,1)S(1)}, f32[...) custom-call(f32[128,256]{1,0:T(8,128)} %bitcast.11, f32[128,256]{1,0:T(8,128)} %bitcast.12, ...), custom_call_target="tpu_custom_call" | custom-call | tf_op jit(solution)/shard_map/pallas_call | solution.py:451
  2.0 23.0 %all_to_all.26.in_ref = f32[32,16,128]{2,1,0:T(8,128)S(1)} all-to-all(f32[32,16,128]{2,1,0:T(8,128)S(1)} %get-tuple-element.18), channel_id=1, replica_groups=mesh['coil'=8,'slab'=32] {'slab'}, dimensions={0} | all-to-all | bytes 524288 | tf_op jit(solution)/shard_map/all_to_all | solution.py:454
  25.0 1.5 %shard_map.65 = (f32[32,16,128]{2,1,0:T(8,128)S(1)}, f32[512,512]{1,0:T(8,128)S(1)}, f32[8,128]{1,0:T(8,128)S(1)}, f32[256,512]{1,0:T(8,128)S(1)}) custom-call(f32[32,16,128]{2,1,0:T(8,128)S(1)} %all_to_all.26.in_ref, f32[1024,128]{1,0:T(8,128)S(1)} %get-tuple-element.19.kernel_ref, bf16[1024,512]{1,0:T(8,128)(2,1)S(1)} %get-tuple-element.20.rows_ref), custom_call_target="tpu_custom_call" | custom-call | tf_op jit(solution)/shard_map/pallas_call | solution.py:456
  26.5 15.0 %all_to_all.27.in_ref = f32[32,16,128]{2,1,0:T(8,128)S(1)} all-to-all(f32[32,16,128]{2,1,0:T(8,128)S(1)} %get-tuple-element.21), channel_id=1, replica_groups=mesh['coil'=8,'slab'=32] {'slab'}, dimensions={0} | all-to-all | bytes 524288 | tf_op jit(solution)/shard_map/all_to_all | solution.py:457
  41.5 0.6 shard_map.66.own_ref
  42.1 1.3 %collective-permute-start = (f32[128,256]{1,0:T(8,128)S(1)}, f32[128,256]{1,0:T(8,128)S(1)}, u32[]{:S(2)}, u32[]{:S(2)}) collective-permute-start(f32[128,256]{1,0:T(8,128)S(1)} %shard_map.66.own_ref), channel_id=1, source_target_pairs={{0,64},{32,96},{64,128},{96,160},{128,192},{160,224},{192,0},{224,... | collective-permute-start | bytes 393224 | tf_op jit(solution)/shard_map/ppermute | solution.py:466
  43.4 2.5 %collective-permute-start.1 = (f32[128,256]{1,0:T(8,128)S(1)}, f32[128,256]{1,0:T(8,128)S(1)}, u32[]{:S(2)}, u32[]{:S(2)}) collective-permute-start(f32[128,256]{1,0:T(8,128)S(1)} %shard_map.66.own_ref), channel_id=1, source_target_pairs={{0,128},{32,160},{64,192},{96,224},{128,0},{160,32},{192,64},{224,... | collective-permute-start | bytes 393224 | tf_op jit(solution)/shard_map/ppermute | solution.py:466
  45.9 1.2 %collective-permute-start.2 = (f32[128,256]{1,0:T(8,128)S(1)}, f32[128,256]{1,0:T(8,128)S(1)}, u32[]{:S(2)}, u32[]{:S(2)}) collective-permute-start(f32[128,256]{1,0:T(8,128)S(1)} %shard_map.66.own_ref), channel_id=1, source_target_pairs={{0,192},{32,224},{64,0},{96,32},{128,64},{160,96},{192,128},{224,1... | collective-permute-start | bytes 393224 | tf_op jit(solution)/shard_map/ppermute | solution.py:466
  47.0 0.2 collective-permute-done.next_ref
  47.2 2.4 %collective-permute-done.1.across_ref = f32[128,256]{1,0:T(8,128)S(1)} collective-permute-done((f32[128,256]{1,0:T(8,128)S(1)}, f32[128,256]{1,0:T(8,128)S(1)}, u32[]{:S(2)}, u32[]{:S(2)}) %collective-permute-start.1) | collective-permute-done | bytes 131104 | tf_op jit(solution)/shard_map/ppermute | solution.py:466
  49.6 0.1 collective-permute-done.2.last_ref
  49.7 5.6 %collective-permute-start.3 = (f32[128,256]{1,0:T(8,128)S(1)}, f32[128,256]{1,0:T(8,128)S(1)}, u32[]{:S(2)}, u32[]{:S(2)}) collective-permute-start(f32[128,256]{1,0:T(8,128)S(1)} %shard_map.67.one_ref), channel_id=1, source_target_pairs={{0,32},{32,0},{64,96},{96,64},{128,160},{160,128},{192,224},{224,1... | collective-permute-start | bytes 393224 | tf_op jit(solution)/shard_map/ppermute | solution.py:470
  55.9 0.3 collective-permute-done.3.other_ref
  56.3 0.6 shard_map.68
  56.9 14.7 %all_to_all.28.in_ref = f32[32,16,128]{2,1,0:T(8,128)S(1)} all-to-all(f32[32,16,128]{2,1,0:T(8,128)S(1)} %get-tuple-element.25), channel_id=1, replica_groups=mesh['coil'=8,'slab'=32] {'slab'}, dimensions={0} | all-to-all | bytes 524288 | tf_op jit(solution)/shard_map/all_to_all | solution.py:474
  71.5 1.2 %shard_map.69 = f32[256,128]{1,0:T(8,128)S(1)} custom-call(f32[32,16,128]{2,1,0:T(8,128)S(1)} %all_to_all.28.in_ref, f32[512,512]{1,0:T(8,128)S(1)} %get-tuple-element.26.before_ref, f32[8,128]{1,0:T(8,128)S(1)} %get-tuple-element.27.energy_ref, f32[8,128]{1,0:T(8,128)S(1)} %get-tuple-element.28.sums_ref, f32[256,512]{1,0:T(8,128)S(1)} %get-tuple-element.29.by_depth_ref, ...), custom_call_target="tpu_custom_call" | custom-call | tf_op jit(solution)/shard_map/pallas_call | solution.py:475
  72.7 20.8 %all_to_all.29 = f32[256,1,128]{2,1,0:T(1,128)S(1)} all-to-all(f32[256,1,128]{2,1,0:T(1,128)S(1)} %bitcast.8), channel_id=1, replica_groups=mesh['coil'=8,'slab'=32] {'coil','slab'}, dimensions={0} | all-to-all | bytes 262144 | tf_op jit(solution)/shard_map/all_to_all | solution.py:478
  93.6 1.0 %shard_map.70 = f32[128,256]{1,0:T(8,128)} custom-call(f32[1]{0:T(128)S(6)} %copy.8.lam_ref, f32[256,128]{1,0:T(8,128)S(1)} %bitcast.9, f32[128,256]{1,0:T(8,128)S(1)} %get-tuple-element.24.vec_ref, f32[128,256]{1,0:T(8,128)S(1)} %get-tuple-element.30.image_ref), custom_call_target="tpu_custom_call" | custom-call | tf_op jit(solution)/shard_map/pallas_call | solution.py:479
  (1 shorter events, 0.0 us)
Async XLA Ops:
  42.1 5.1 %collective-permute-start = (f32[128,256]{1,0:T(8,128)S(1)}, f32[128,256]{1,0:T(8,128)S(1)}, u32[]{:S(2)}, u32[]{:S(2)}) collective-permute-start(f32[128,256]{1,0:T(8,128)S(1)} %shard_map.66.own_ref), channel_id=1, source_target_pairs={{0,64},{32,96},{64,128},{96,160},{128,192},{160,224},{192,0},{224,... | collective-permute-start | bytes 393224 | tf_op jit(solution)/shard_map/ppermute | solution.py:466
  43.4 6.2 %collective-permute-start.1 = (f32[128,256]{1,0:T(8,128)S(1)}, f32[128,256]{1,0:T(8,128)S(1)}, u32[]{:S(2)}, u32[]{:S(2)}) collective-permute-start(f32[128,256]{1,0:T(8,128)S(1)} %shard_map.66.own_ref), channel_id=1, source_target_pairs={{0,128},{32,160},{64,192},{96,224},{128,0},{160,32},{192,64},{224,... | collective-permute-start | bytes 393224 | tf_op jit(solution)/shard_map/ppermute | solution.py:466
  45.9 3.8 %collective-permute-start.2 = (f32[128,256]{1,0:T(8,128)S(1)}, f32[128,256]{1,0:T(8,128)S(1)}, u32[]{:S(2)}, u32[]{:S(2)}) collective-permute-start(f32[128,256]{1,0:T(8,128)S(1)} %shard_map.66.own_ref), channel_id=1, source_target_pairs={{0,192},{32,224},{64,0},{96,32},{128,64},{160,96},{192,128},{224,1... | collective-permute-start | bytes 393224 | tf_op jit(solution)/shard_map/ppermute | solution.py:466
  49.7 6.6 %collective-permute-start.3 = (f32[128,256]{1,0:T(8,128)S(1)}, f32[128,256]{1,0:T(8,128)S(1)}, u32[]{:S(2)}, u32[]{:S(2)}) collective-permute-start(f32[128,256]{1,0:T(8,128)S(1)} %shard_map.67.one_ref), channel_id=1, source_target_pairs={{0,32},{32,0},{64,96},{96,64},{128,160},{160,128},{192,224},{224,1... | collective-permute-start | bytes 393224 | tf_op jit(solution)/shard_map/ppermute | solution.py:470
where the time goes:
time: 94.8 us; the launch traced here: 94.6 us
  blocking collectives  73.5 us (78%)
  starting transfers between devices  10.4 us (11%)
  Pallas kernels  6.92 us (7%)
  waiting for transfers between devices  3 us (3%)
    all_to_all x2, blocking collectives, shards(): got = to_slabs(sent)  37.7 us
    all_to_all x1, blocking collectives, shards(): every = lax.all_to_all(own, ('coil', 'slab'), 0, 0, tiled=True)  20.8 us
    all_to_all x1, blocking collectives, shards(): home = to_slabs(back)  15 us
    ppermute x1, starting transfers between devices, shards(): other = lax.ppermute(pair, 'coil', [(at, at ^ 1) for at in range(coils)])  5.57 us
    ppermute x3, starting transfers between devices, from_chip(): return lax.ppermute(term, 'coil', pairs)  4.87 us
    ppermute x3, waiting for transfers between devices, from_chip(): return lax.ppermute(term, 'coil', pairs)  2.66 us
    pallas_call x1, Pallas kernels, shards(): call(start_kernel, [block, *loaded], 'hhhhh', [dma((len(sources) + filt.s...  2 us
  transfers between devices with their start and end apart: 4, of which 4 were waited for; matrix products, arithmetic and copies ran while one was open for 0% of the time, Pallas kernels for 0%

commit v1 on v0

--- a/solution.py
+++ b/solution.py
@@ -34,7 +34,7 @@
 
 def plane_table(length):
     table = dft(length)
-    return np.concatenate([table.real, table.imag], axis=1)
+    return np.concatenate([table.real, table.imag], axis=0)
 
 
 def rows_table(length, slabs, scale):
@@ -94,19 +94,17 @@
             straight_ref[at : at + rows], straight_ref[at + rows : at + 2 * rows] = one, other
             turned_ref[at : at + rows], turned_ref[at + rows : at + 2 * rows] = -other, one
 
-    def by_parity(ref):
-        parts = [
-            jnp.concatenate(
-                [ref[pl.ds(lanes * 2 * cells + parity, cells, stride=2), :] for lanes in range(width // 128)], axis=1
-            )
-            for parity in range(2)
-        ]
-        return split(jnp.concatenate(parts, axis=0))
-
-    straight, turned = by_parity(straight_ref), by_parity(turned_ref)
-    high, low = table()
-    spec = product(straight, (high[:, :grid_size], low[:, :grid_size]), NN)
-    spec = spec + product(turned, (high[:, grid_size:], low[:, grid_size:]), NN)
+    tiled = range(0, width // 128 * 2 * cells, 2 * cells)
+    parts = [
+        jnp.concatenate(
+            [ref[pl.ds(at + parity, cells, stride=2), :] for ref in (straight_ref, turned_ref) for at in tiled], axis=1
+        )
+        for parity in range(2)
+    ]
+    dot = partial(jnp.dot, preferred_element_type=F32)
+    pair = split(jnp.concatenate(parts, axis=0))
+    spec = dot(jnp.concatenate(pair, axis=0), table(0))
+    spec = (spec[: 2 * cells] + spec[2 * cells :]) + dot(pair[0], table(1))
     tiles = [
         jnp.concatenate(
             [
@@ -219,8 +217,11 @@
     count = (len(refs) - 4) // 2
     sources, out_ref, loaded = refs[:count], refs[count], refs[count + 1 : 2 * count + 1]
     sems, *spaces = refs[2 * count + 1 :]
-    pairs = []
-    for source, target in zip(sources, loaded):
+    vec_ref, sens_ref, table_ref = loaded[:3]
+    half = table_ref.shape[0] // 2
+    pairs = [(sources[at], loaded[at]) for at in range(2)]
+    pairs += [(sources[2].at[pl.ds(at, half)], table_ref.at[pl.ds(at, half)]) for at in (0, half)]
+    for source, target in zip(sources[3:], loaded[3:]):
         rows, lanes = source.shape[0], target.shape[1]
         for tile in range(source.shape[1] // lanes):
             pairs.append((source.at[:, pl.ds(tile * lanes, lanes)], target.at[pl.ds(tile * rows, rows)]))
@@ -229,16 +230,15 @@
         copy.start()
     for copy in copies[:2]:
         copy.wait()
-    vec_ref, sens_ref, table_ref = loaded[:3]
     cells = vec_ref.shape[0] // 2
     real, imag = coil_product(sens_ref, vec_ref[:cells], vec_ref[cells:])
 
-    def table():
-        copies[2].wait()
-        return pair_of(table_ref, 0)
+    def table(part):
+        copies[2 + part].wait()
+        return table_ref[part * half : (part + 1) * half]
 
     send_columns(real, imag, table, out_ref, *spaces)
-    for copy in copies[3:]:
+    for copy in copies[4:]:
         copy.wait()
 
 
@@ -296,11 +296,8 @@
         ],
         axis=0,
     )
-    spec = split(spec)
-    grid_size = blocks * 128
-    high, low = pair_of(table_ref, 0)
-    by_real = product(spec, (high[:, :grid_size], low[:, :grid_size]), NT)
-    by_imag = product(spec, (high[:, grid_size:], low[:, grid_size:]), NT)
+    both = product(split(spec), pair_of(table_ref, 0), NT)
+    by_real, by_imag = both[:, : both.shape[1] // 2], both[:, both.shape[1] // 2 :]
     cells = planes * 8
     tiled = range(by_real.shape[1] // 128)
     for parity in range(2):
@@ -324,7 +321,7 @@
     out_ref[cells:] = sens_re * img_im - sens_im * img_re
 
 
-def add_kernel(own_ref, next_ref, across_ref, last_ref, out_ref):
+def add_kernel(own_ref, next_ref, last_ref, across_ref, out_ref):
     out_ref[...] = (own_ref[...] + across_ref[...]) + (next_ref[...] + last_ref[...])
 
 
@@ -337,7 +334,7 @@
     image = (one_ref[...] + other_ref[...]) + lam_ref[0] * vec
     image_ref[...] = image
     real, imag = coil_product(sens_ref, image[:cells], image[cells:])
-    send_columns(real, imag, partial(pair_of, table_ref, 0), out_ref, straight_ref, turned_ref)
+    send_columns(real, imag, pair_of(table_ref, 0).__getitem__, out_ref, straight_ref, turned_ref)
     norm = total(vec * vec)
     ratio = along(total(vec * image), norm)
     rest = image - ratio * vec
@@ -449,7 +446,7 @@
     loaded = [pltpu.VMEM(array.shape, array.dtype) for array in sources]
     loaded[3] = pltpu.VMEM((filt.size // 128, 128), F32)
     sent, vec, sens, table, filt, row_table = call(
-        start_kernel, [block, *loaded], "hhhhh", [dma((len(sources) + filt.shape[1] // 128 - 1,)), *spaces]
+        start_kernel, [block, *loaded], "hhhhh", [dma((len(sources) + filt.shape[1] // 128,)), *spaces]
     )(*sources)
     got = to_slabs(sent)
     shapes = [block, (4 * lanes, 2 * width), (8, 128), (2 * lanes, 2 * width)]
@@ -465,8 +462,7 @@
         ]
         return lax.ppermute(term, "coil", pairs)
 
-    across = from_chip(2)
-    pair = call(add_kernel, [term.shape], "vvvv")(term, from_chip(1), across, from_chip(3))
+    pair = call(add_kernel, [term.shape], "vvvv")(term, *[from_chip(shift) for shift in (1, 3, 2)])
     other = lax.ppermute(pair, "coil", [(at, at ^ 1) for at in range(coils)])
     sent, image, sums = call(turn_kernel, [block, (cells2, width), (8, 128)], "svvvvv", spaces)(
         reg_weight, pair, other, vec, sens, table

time: 94.8 us -> 94.4 us (level)
  waiting for transfers between devices: 3 us -> 4.14 us
    ppermute x3, waiting for transfers between devices: 2.66 us -> 3.8 us  [from_chip(): return lax.ppermute(term, 'coil', pairs)]
  transfers between devices with their start and end apart: 4 -> 4, of which waited for: 4 -> 3; matrix products, arithmetic and copies ran while one was open for 0% -> 0% of each run, Pallas kernels for 0% -> 0%
where the time goes in v1:
time: 94.4 us; the launch traced here: 94.2 us
  blocking collectives  72.7 us (77%)
  starting transfers between devices  9.83 us (10%)
  Pallas kernels  6.81 us (7%)
  waiting for transfers between devices  4.14 us (4%)
    all_to_all x2, blocking collectives, shards(): got = to_slabs(sent)  37.7 us
    all_to_all x1, blocking collectives, shards(): every = lax.all_to_all(own, ('coil', 'slab'), 0, 0, tiled=True)  20 us
    all_to_all x1, blocking collectives, shards(): home = to_slabs(back)  15 us
    ppermute x1, starting transfers between devices, shards(): other = lax.ppermute(pair, 'coil', [(at, at ^ 1) for at in range(coils)])  5.54 us
    ppermute x3, starting transfers between devices, from_chip(): return lax.ppermute(term, 'coil', pairs)  4.29 us
    ppermute x3, waiting for transfers between devices, from_chip(): return lax.ppermute(term, 'coil', pairs)  3.8 us
    pallas_call x1, Pallas kernels, shards(): call(start_kernel, [block, *loaded], 'hhhhh', [dma((len(sources) + filt.s...  1.93 us
  transfers between devices with their start and end apart: 4, of which 3 were waited for; matrix products, arithmetic and copies ran while one was open for 0% of the time, Pallas kernels for 0%

profile of v1, /device:TPU:1, one launch (start us, length us, event | category | flops | bytes accessed | tf_op | source)
XLA Modules:
  0.0 94.2 jit_solution(3182718914156316049)
XLA Ops:
  0.0 1.9 %shard_map.64 = (f32[32,16,128]{2,1,0:T(8,128)S(1)}, f32[128,256]{1,0:T(8,128)S(1)}, f32[128,256]{1,0:T(8,128)S(1)}, bf16[1024,512]{1,0:T(8,128)(2,1)S(1)}, f32[...) custom-call(f32[128,256]{1,0:T(8,128)} %bitcast.11, f32[128,256]{1,0:T(8,128)} %bitcast.12, ...), custom_call_target="tpu_custom_call" | custom-call | tf_op jit(solution)/shard_map/pallas_call | solution.py:448
  1.9 23.0 %all_to_all.26.in_ref = f32[32,16,128]{2,1,0:T(8,128)S(1)} all-to-all(f32[32,16,128]{2,1,0:T(8,128)S(1)} %get-tuple-element.18), channel_id=1, replica_groups=mesh['coil'=8,'slab'=32] {'slab'}, dimensions={0} | all-to-all | bytes 524288 | tf_op jit(solution)/shard_map/all_to_all | solution.py:451
  25.0 1.5 %shard_map.65 = (f32[32,16,128]{2,1,0:T(8,128)S(1)}, f32[512,512]{1,0:T(8,128)S(1)}, f32[8,128]{1,0:T(8,128)S(1)}, f32[256,512]{1,0:T(8,128)S(1)}) custom-call(f32[32,16,128]{2,1,0:T(8,128)S(1)} %all_to_all.26.in_ref, f32[1024,128]{1,0:T(8,128)S(1)} %get-tuple-element.19.kernel_ref, bf16[1024,512]{1,0:T(8,128)(2,1)S(1)} %get-tuple-element.20.rows_ref), custom_call_target="tpu_custom_call" | custom-call | tf_op jit(solution)/shard_map/pallas_call | solution.py:453
  26.5 15.0 %all_to_all.27.in_ref = f32[32,16,128]{2,1,0:T(8,128)S(1)} all-to-all(f32[32,16,128]{2,1,0:T(8,128)S(1)} %get-tuple-element.21), channel_id=1, replica_groups=mesh['coil'=8,'slab'=32] {'slab'}, dimensions={0} | all-to-all | bytes 524288 | tf_op jit(solution)/shard_map/all_to_all | solution.py:454
  41.4 0.6 shard_map.66.own_ref
  42.0 1.3 %collective-permute-start = (f32[128,256]{1,0:T(8,128)S(1)}, f32[128,256]{1,0:T(8,128)S(1)}, u32[]{:S(2)}, u32[]{:S(2)}) collective-permute-start(f32[128,256]{1,0:T(8,128)S(1)} %shard_map.66.own_ref), channel_id=1, source_target_pairs={{0,64},{32,96},{64,128},{96,160},{128,192},{160,224},{192,0},{224,... | collective-permute-start | bytes 393224 | tf_op jit(solution)/shard_map/ppermute | solution.py:463
  43.3 1.5 %collective-permute-start.1 = (f32[128,256]{1,0:T(8,128)S(1)}, f32[128,256]{1,0:T(8,128)S(1)}, u32[]{:S(2)}, u32[]{:S(2)}) collective-permute-start(f32[128,256]{1,0:T(8,128)S(1)} %shard_map.66.own_ref), channel_id=1, source_target_pairs={{0,192},{32,224},{64,0},{96,32},{128,64},{160,96},{192,128},{224,1... | collective-permute-start | bytes 393224 | tf_op jit(solution)/shard_map/ppermute | solution.py:463
  44.8 1.5 %collective-permute-start.2 = (f32[128,256]{1,0:T(8,128)S(1)}, f32[128,256]{1,0:T(8,128)S(1)}, u32[]{:S(2)}, u32[]{:S(2)}) collective-permute-start(f32[128,256]{1,0:T(8,128)S(1)} %shard_map.66.own_ref), channel_id=1, source_target_pairs={{0,128},{32,160},{64,192},{96,224},{128,0},{160,32},{192,64},{224,... | collective-permute-start | bytes 393224 | tf_op jit(solution)/shard_map/ppermute | solution.py:463
  46.3 0.8 collective-permute-done.next_ref
  47.1 0.0 collective-permute-done.1.last_ref
  47.2 3.0 %collective-permute-done.2.across_ref = f32[128,256]{1,0:T(8,128)S(1)} collective-permute-done((f32[128,256]{1,0:T(8,128)S(1)}, f32[128,256]{1,0:T(8,128)S(1)}, u32[]{:S(2)}, u32[]{:S(2)}) %collective-permute-start.2) | collective-permute-done | bytes 131104 | tf_op jit(solution)/shard_map/ppermute | solution.py:463
  50.2 5.5 %collective-permute-start.3 = (f32[128,256]{1,0:T(8,128)S(1)}, f32[128,256]{1,0:T(8,128)S(1)}, u32[]{:S(2)}, u32[]{:S(2)}) collective-permute-start(f32[128,256]{1,0:T(8,128)S(1)} %shard_map.67.one_ref), channel_id=1, source_target_pairs={{0,32},{32,0},{64,96},{96,64},{128,160},{160,128},{192,224},{224,1... | collective-permute-start | bytes 393224 | tf_op jit(solution)/shard_map/ppermute | solution.py:466
  56.3 0.3 collective-permute-done.3.other_ref
  56.7 0.6 shard_map.68
  57.3 14.7 %all_to_all.28.in_ref = f32[32,16,128]{2,1,0:T(8,128)S(1)} all-to-all(f32[32,16,128]{2,1,0:T(8,128)S(1)} %get-tuple-element.25), channel_id=1, replica_groups=mesh['coil'=8,'slab'=32] {'slab'}, dimensions={0} | all-to-all | bytes 524288 | tf_op jit(solution)/shard_map/all_to_all | solution.py:470
  72.0 1.2 %shard_map.69 = f32[256,128]{1,0:T(8,128)S(1)} custom-call(f32[32,16,128]{2,1,0:T(8,128)S(1)} %all_to_all.28.in_ref, f32[512,512]{1,0:T(8,128)S(1)} %get-tuple-element.26.before_ref, f32[8,128]{1,0:T(8,128)S(1)} %get-tuple-element.27.energy_ref, f32[8,128]{1,0:T(8,128)S(1)} %get-tuple-element.28.sums_ref, f32[256,512]{1,0:T(8,128)S(1)} %get-tuple-element.29.by_depth_ref, ...), custom_call_target="tpu_custom_call" | custom-call | tf_op jit(solution)/shard_map/pallas_call | solution.py:471
  73.2 20.0 %all_to_all.29 = f32[256,1,128]{2,1,0:T(1,128)S(1)} all-to-all(f32[256,1,128]{2,1,0:T(1,128)S(1)} %bitcast.8), channel_id=1, replica_groups=mesh['coil'=8,'slab'=32] {'coil','slab'}, dimensions={0} | all-to-all | bytes 262144 | tf_op jit(solution)/shard_map/all_to_all | solution.py:474
  93.2 1.0 %shard_map.70 = f32[128,256]{1,0:T(8,128)} custom-call(f32[1]{0:T(128)S(6)} %copy.8.lam_ref, f32[256,128]{1,0:T(8,128)S(1)} %bitcast.9, f32[128,256]{1,0:T(8,128)S(1)} %get-tuple-element.24.vec_ref, f32[128,256]{1,0:T(8,128)S(1)} %get-tuple-element.30.image_ref), custom_call_target="tpu_custom_call" | custom-call | tf_op jit(solution)/shard_map/pallas_call | solution.py:475
  (1 shorter events, 0.0 us)
Async XLA Ops:
  42.0 5.1 %collective-permute-start = (f32[128,256]{1,0:T(8,128)S(1)}, f32[128,256]{1,0:T(8,128)S(1)}, u32[]{:S(2)}, u32[]{:S(2)}) collective-permute-start(f32[128,256]{1,0:T(8,128)S(1)} %shard_map.66.own_ref), channel_id=1, source_target_pairs={{0,64},{32,96},{64,128},{96,160},{128,192},{160,224},{192,0},{224,... | collective-permute-start | bytes 393224 | tf_op jit(solution)/shard_map/ppermute | solution.py:463
  43.3 3.8 %collective-permute-start.1 = (f32[128,256]{1,0:T(8,128)S(1)}, f32[128,256]{1,0:T(8,128)S(1)}, u32[]{:S(2)}, u32[]{:S(2)}) collective-permute-start(f32[128,256]{1,0:T(8,128)S(1)} %shard_map.66.own_ref), channel_id=1, source_target_pairs={{0,192},{32,224},{64,0},{96,32},{128,64},{160,96},{192,128},{224,1... | collective-permute-start | bytes 393224 | tf_op jit(solution)/shard_map/ppermute | solution.py:463
  44.8 5.3 %collective-permute-start.2 = (f32[128,256]{1,0:T(8,128)S(1)}, f32[128,256]{1,0:T(8,128)S(1)}, u32[]{:S(2)}, u32[]{:S(2)}) collective-permute-start(f32[128,256]{1,0:T(8,128)S(1)} %shard_map.66.own_ref), channel_id=1, source_target_pairs={{0,128},{32,160},{64,192},{96,224},{128,0},{160,32},{192,64},{224,... | collective-permute-start | bytes 393224 | tf_op jit(solution)/shard_map/ppermute | solution.py:463
  50.2 6.5 %collective-permute-start.3 = (f32[128,256]{1,0:T(8,128)S(1)}, f32[128,256]{1,0:T(8,128)S(1)}, u32[]{:S(2)}, u32[]{:S(2)}) collective-permute-start(f32[128,256]{1,0:T(8,128)S(1)} %shard_map.67.one_ref), channel_id=1, source_target_pairs={{0,32},{32,0},{64,96},{96,64},{128,160},{160,128},{192,224},{224,1... | collective-permute-start | bytes 393224 | tf_op jit(solution)/shard_map/ppermute | solution.py:466

commit v2 on v1

--- a/solution.py
+++ b/solution.py
@@ -214,9 +214,9 @@
 
 
 def start_kernel(*refs):
-    count = (len(refs) - 4) // 2
-    sources, out_ref, loaded = refs[:count], refs[count], refs[count + 1 : 2 * count + 1]
-    sems, *spaces = refs[2 * count + 1 :]
+    count = (len(refs) - 7) // 2
+    sources, core_hbm, out_ref, loaded = refs[:count], refs[count], refs[count + 1], refs[count + 2 : 2 * count + 2]
+    core_ref, sems, core_smem, *spaces = refs[2 * count + 2 :]
     vec_ref, sens_ref, table_ref = loaded[:3]
     half = table_ref.shape[0] // 2
     pairs = [(sources[at], loaded[at]) for at in range(2)]
@@ -225,6 +225,7 @@
         rows, lanes = source.shape[0], target.shape[1]
         for tile in range(source.shape[1] // lanes):
             pairs.append((source.at[:, pl.ds(tile * lanes, lanes)], target.at[pl.ds(tile * rows, rows)]))
+    pairs.append((core_hbm, core_smem))
     copies = [pltpu.make_async_copy(*pair, sems.at[at]) for at, pair in enumerate(pairs)]
     for copy in copies:
         copy.start()
@@ -240,6 +241,7 @@
     send_columns(real, imag, table, out_ref, *spaces)
     for copy in copies[4:]:
         copy.wait()
+    core_ref[...] = jnp.full(core_ref.shape, core_smem[0], F32)
 
 
 def filter_kernel(in_ref, kernel_ref, rows_ref, out_ref, spec_ref, energy_ref, by_depth_ref):
@@ -321,17 +323,41 @@
     out_ref[cells:] = sens_re * img_im - sens_im * img_re
 
 
-def add_kernel(own_ref, next_ref, last_ref, across_ref, out_ref):
-    out_ref[...] = (own_ref[...] + across_ref[...]) + (next_ref[...] + last_ref[...])
+def is_first(core_ref, shape):
+    return jnp.broadcast_to(core_ref[0:1, 0:1], shape) == 0.0
+
+
+def pair_kernel(core_ref, own_ref, other_ref, out_ref, half_ref):
+    rows = half_ref.shape[0]
+    both = own_ref[...] + other_ref[...]
+    out_ref[...] = both
+    half_ref[...] = jnp.where(is_first(core_ref, half_ref.shape), both[:rows], both[rows:])
 
 
 def turn_kernel(
-    lam_ref, one_ref, other_ref, vec_ref, sens_ref, table_ref, out_ref, image_ref, sums_ref, straight_ref, turned_ref
+    core_ref,
+    lam_ref,
+    pair_ref,
+    near_ref,
+    other_near_ref,
+    far_ref,
+    other_far_ref,
+    vec_ref,
+    sens_ref,
+    table_ref,
+    out_ref,
+    image_ref,
+    sums_ref,
+    straight_ref,
+    turned_ref,
 ):
     cells2, width = vec_ref.shape
     cells = cells2 // 2
     vec = vec_ref[...]
-    image = (one_ref[...] + other_ref[...]) + lam_ref[0] * vec
+    first = is_first(core_ref, far_ref.shape)
+    far, other_far = far_ref[...], other_far_ref[...]
+    across = jnp.concatenate([jnp.where(first, far, other_far), jnp.where(first, other_far, far)], axis=0)
+    image = ((pair_ref[...] + across) + (near_ref[...] + other_near_ref[...])) + lam_ref[0] * vec
     image_ref[...] = image
     real, imag = coil_product(sens_ref, image[:cells], image[cells:])
     send_columns(real, imag, pair_of(table_ref, 0).__getitem__, out_ref, straight_ref, turned_ref)
@@ -437,6 +463,7 @@
     table = halves(plane_table(width), 0)
     row_table = halves(rows_table(width, slabs, 1.0 / math.sqrt(2 * planes)), 0)
     lanes = planes * cols
+    core = (lax.axis_index("coil") % 2).astype(F32).reshape(1)
     block = (slabs, 2 * rows, lanes)
     to_slabs = partial(lax.all_to_all, axis_name="slab", split_axis=0, concat_axis=0, tiled=True)
     dma = pltpu.SemaphoreType.DMA
@@ -445,9 +472,14 @@
     sources = [pltpu.with_memory_space_constraint(array, pltpu.HBM) for array in (vec, sens, table, filt, row_table)]
     loaded = [pltpu.VMEM(array.shape, array.dtype) for array in sources]
     loaded[3] = pltpu.VMEM((filt.size // 128, 128), F32)
-    sent, vec, sens, table, filt, row_table = call(
-        start_kernel, [block, *loaded], "hhhhh", [dma((len(sources) + filt.shape[1] // 128,)), *spaces]
-    )(*sources)
+    core = pltpu.with_memory_space_constraint(core, pltpu.HBM)
+    sems = dma((len(sources) + filt.shape[1] // 128 + 1,))
+    sent, vec, sens, table, filt, row_table, core = call(
+        start_kernel,
+        [block, *loaded, pltpu.VMEM((8, 128), F32)],
+        "hhhhhh",
+        [sems, pltpu.SMEM((1,), F32), *spaces],
+    )(*sources, core)
     got = to_slabs(sent)
     shapes = [block, (4 * lanes, 2 * width), (8, 128), (2 * lanes, 2 * width)]
     back, before, energy_now, filt = call(filter_kernel, shapes, "vvv", (), 32)(got, filt, row_table)
@@ -456,16 +488,17 @@
 
     chips = coils // 2
 
-    def from_chip(shift):
+    def moved(values, core_flip, *shifts):
         pairs = [
-            (2 * chip + core, 2 * ((chip + shift) % chips) + core) for chip in range(chips) for core in range(2)
+            (2 * chip + at, 2 * ((chip + shifts[at]) % chips) + (at ^ core_flip)) for chip in range(chips) for at in (0, 1)
         ]
-        return lax.ppermute(term, "coil", pairs)
-
-    pair = call(add_kernel, [term.shape], "vvvv")(term, *[from_chip(shift) for shift in (1, 3, 2)])
-    other = lax.ppermute(pair, "coil", [(at, at ^ 1) for at in range(coils)])
-    sent, image, sums = call(turn_kernel, [block, (cells2, width), (8, 128)], "svvvvv", spaces)(
-        reg_weight, pair, other, vec, sens, table
+        return lax.ppermute(values, "coil", pairs)
+
+    halves_of = [pltpu.VMEM((cells2, width), F32), pltpu.VMEM((cells2 // 2, width), F32)]
+    pair, half = call(pair_kernel, halves_of, "vvv")(core, term, moved(term, 1, 0, 0))
+    near, far = moved(pair, 0, 1, chips - 1), moved(half, 0, 2, 2)
+    sent, image, sums = call(turn_kernel, [block, (cells2, width), (8, 128)], "vsvvvvvvvv", spaces)(
+        core, reg_weight, pair, near, moved(near, 1, 0, 0), far, moved(far, 1, 0, 0), vec, sens, table
     )
     got = to_slabs(sent)
     own = call(last_kernel, [(coils * slabs, 128)], "vvvvvv", (), 32)(

time: 94.4 us -> 94.4 us (level)
  waiting for transfers between devices: 4.14 us -> 5.58 us
  starting transfers between devices: 9.83 us -> 8.52 us
    ppermute x4 -> x5, waiting for transfers between devices: 4.14 us -> 5.58 us  [moved(): return lax.ppermute(values, 'coil', pairs)]
    ppermute x4 -> x5, starting transfers between devices: 9.83 us -> 8.52 us  [moved(): return lax.ppermute(values, 'coil', pairs)]
  transfers between devices with their start and end apart: 4 -> 5, of which waited for: 3 -> 4; matrix products, arithmetic and copies ran while one was open for 0% -> 0% of each run, Pallas kernels for 0% -> 0%
where the time goes in v2:
time: 94.4 us; the launch traced here: 94.1 us
  blocking collectives  72.4 us (77%)
  starting transfers between devices  8.52 us (9%)
  Pallas kernels  6.9 us (7%)
  waiting for transfers between devices  5.58 us (6%)
    all_to_all x2, blocking collectives, shards(): got = to_slabs(sent)  37.7 us
    all_to_all x1, blocking collectives, shards(): every = lax.all_to_all(own, ('coil', 'slab'), 0, 0, tiled=True)  19.7 us
    all_to_all x1, blocking collectives, shards(): home = to_slabs(back)  15 us
    ppermute x5, starting transfers between devices, moved(): return lax.ppermute(values, 'coil', pairs)  8.52 us
    ppermute x5, waiting for transfers between devices, moved(): return lax.ppermute(values, 'coil', pairs)  5.58 us
    pallas_call x1, Pallas kernels, shards(): call(start_kernel, [block, *loaded, pltpu.VMEM((8, 128), F32)], 'hhhhhh',...  1.95 us
  transfers between devices with their start and end apart: 5, of which 4 were waited for; matrix products, arithmetic and copies ran while one was open for 0% of the time, Pallas kernels for 0%

profile of v2, /device:TPU:1, one launch (start us, length us, event | category | flops | bytes accessed | tf_op | source)
XLA Modules:
  0.0 94.1 jit_solution(8272763710754005417)
XLA Ops:
  0.0 1.9 %shard_map.64 = (f32[32,16,128]{2,1,0:T(8,128)S(1)}, f32[128,256]{1,0:T(8,128)S(1)}, f32[128,256]{1,0:T(8,128)S(1)}, bf16[1024,512]{1,0:T(8,128)(2,1)S(1)}, f32[...) custom-call(f32[128,256]{1,0:T(8,128)} %bitcast.12, f32[128,256]{1,0:T(8,128)} %bitcast.13, ...), custom_call_target="tpu_custom_call" | custom-call | tf_op jit(solution)/shard_map/pallas_call | solution.py:477
  2.0 23.0 %all_to_all.26.in_ref = f32[32,16,128]{2,1,0:T(8,128)S(1)} all-to-all(f32[32,16,128]{2,1,0:T(8,128)S(1)} %get-tuple-element.22), channel_id=1, replica_groups=mesh['coil'=8,'slab'=32] {'slab'}, dimensions={0} | all-to-all | bytes 524288 | tf_op jit(solution)/shard_map/all_to_all | solution.py:483
  25.0 1.5 %shard_map.65 = (f32[32,16,128]{2,1,0:T(8,128)S(1)}, f32[512,512]{1,0:T(8,128)S(1)}, f32[8,128]{1,0:T(8,128)S(1)}, f32[256,512]{1,0:T(8,128)S(1)}) custom-call(f32[32,16,128]{2,1,0:T(8,128)S(1)} %all_to_all.26.in_ref, f32[1024,128]{1,0:T(8,128)S(1)} %get-tuple-element.23.kernel_ref, bf16[1024,512]{1,0:T(8,128)(2,1)S(1)} %get-tuple-element.24.rows_ref), custom_call_target="tpu_custom_call" | custom-call | tf_op jit(solution)/shard_map/pallas_call | solution.py:485
  26.5 15.0 %all_to_all.27.in_ref = f32[32,16,128]{2,1,0:T(8,128)S(1)} all-to-all(f32[32,16,128]{2,1,0:T(8,128)S(1)} %get-tuple-element.25), channel_id=1, replica_groups=mesh['coil'=8,'slab'=32] {'slab'}, dimensions={0} | all-to-all | bytes 524288 | tf_op jit(solution)/shard_map/all_to_all | solution.py:486
  41.5 0.6 shard_map.66.own_ref
  42.1 3.9 %collective-permute-start = (f32[128,256]{1,0:T(8,128)S(1)}, f32[128,256]{1,0:T(8,128)S(1)}, u32[]{:S(2)}, u32[]{:S(2)}) collective-permute-start(f32[128,256]{1,0:T(8,128)S(1)} %shard_map.66.own_ref), channel_id=1, source_target_pairs={{0,32},{32,0},{64,96},{96,64},{128,160},{160,128},{192,224},{224,1... | collective-permute-start | bytes 393224 | tf_op jit(solution)/shard_map/ppermute | solution.py:495
  45.9 1.0 %collective-permute-done.other_ref = f32[128,256]{1,0:T(8,128)S(1)} collective-permute-done((f32[128,256]{1,0:T(8,128)S(1)}, f32[128,256]{1,0:T(8,128)S(1)}, u32[]{:S(2)}, u32[]{:S(2)}) %collective-permute-start) | collective-permute-done | bytes 131104 | tf_op jit(solution)/shard_map/ppermute | solution.py:495
  46.9 0.1 shard_map.67
  47.0 2.6 %collective-permute-start.1 = (f32[128,256]{1,0:T(8,128)S(1)}, f32[128,256]{1,0:T(8,128)S(1)}, u32[]{:S(2)}, u32[]{:S(2)}) collective-permute-start(f32[128,256]{1,0:T(8,128)S(1)} %get-tuple-element.28.pair_ref), channel_id=1, source_target_pairs={{0,64},{32,224},{64,128},{96,32},{128,192},{160,96},{192,0},{224,1... | collective-permute-start | bytes 393224 | tf_op jit(solution)/shard_map/ppermute | solution.py:495
  49.5 0.5 collective-permute-start.3
  50.0 2.8 %collective-permute-done.1.near_ref = f32[128,256]{1,0:T(8,128)S(1)} collective-permute-done((f32[128,256]{1,0:T(8,128)S(1)}, f32[128,256]{1,0:T(8,128)S(1)}, u32[]{:S(2)}, u32[]{:S(2)}) %collective-permute-start.1) | collective-permute-done | bytes 131104 | tf_op jit(solution)/shard_map/ppermute | solution.py:495
  52.8 0.7 collective-permute-start.2
  53.6 1.6 %collective-permute-done.3.far_ref = f32[64,256]{1,0:T(8,128)S(1)} collective-permute-done((f32[64,256]{1,0:T(8,128)S(1)}, f32[64,256]{1,0:T(8,128)S(1)}, u32[]{:S(2)}, u32[]{:S(2)}) %collective-permute-start.3) | collective-permute-done | bytes 65568 | tf_op jit(solution)/shard_map/ppermute | solution.py:495
  55.1 0.8 collective-permute-start.4
  56.6 0.3 collective-permute-done.4.other_far_ref
  56.9 0.0 collective-permute-done.2.other_near_ref
  56.9 0.6 shard_map.68
  57.5 14.7 %all_to_all.28.in_ref = f32[32,16,128]{2,1,0:T(8,128)S(1)} all-to-all(f32[32,16,128]{2,1,0:T(8,128)S(1)} %get-tuple-element.31), channel_id=1, replica_groups=mesh['coil'=8,'slab'=32] {'slab'}, dimensions={0} | all-to-all | bytes 524288 | tf_op jit(solution)/shard_map/all_to_all | solution.py:503
  72.2 1.2 %shard_map.69 = f32[256,128]{1,0:T(8,128)S(1)} custom-call(f32[32,16,128]{2,1,0:T(8,128)S(1)} %all_to_all.28.in_ref, f32[512,512]{1,0:T(8,128)S(1)} %get-tuple-element.32.before_ref, f32[8,128]{1,0:T(8,128)S(1)} %get-tuple-element.33.energy_ref, f32[8,128]{1,0:T(8,128)S(1)} %get-tuple-element.34.sums_ref, f32[256,512]{1,0:T(8,128)S(1)} %get-tuple-element.35.by_depth_ref, ...), custom_call_target="tpu_custom_call" | custom-call | tf_op jit(solution)/shard_map/pallas_call | solution.py:504
  73.4 19.7 %all_to_all.29 = f32[256,1,128]{2,1,0:T(1,128)S(1)} all-to-all(f32[256,1,128]{2,1,0:T(1,128)S(1)} %bitcast.9), channel_id=1, replica_groups=mesh['coil'=8,'slab'=32] {'coil','slab'}, dimensions={0} | all-to-all | bytes 262144 | tf_op jit(solution)/shard_map/all_to_all | solution.py:507
  93.1 1.0 %shard_map.70 = f32[128,256]{1,0:T(8,128)} custom-call(f32[1]{0:T(128)S(6)} %copy.8.lam_ref, f32[256,128]{1,0:T(8,128)S(1)} %bitcast.10, f32[128,256]{1,0:T(8,128)S(1)} %get-tuple-element.30.vec_ref, f32[128,256]{1,0:T(8,128)S(1)} %get-tuple-element.36.image_ref), custom_call_target="tpu_custom_call" | custom-call | tf_op jit(solution)/shard_map/pallas_call | solution.py:508
Async XLA Ops:
  42.1 4.8 %collective-permute-start = (f32[128,256]{1,0:T(8,128)S(1)}, f32[128,256]{1,0:T(8,128)S(1)}, u32[]{:S(2)}, u32[]{:S(2)}) collective-permute-start(f32[128,256]{1,0:T(8,128)S(1)} %shard_map.66.own_ref), channel_id=1, source_target_pairs={{0,32},{32,0},{64,96},{96,64},{128,160},{160,128},{192,224},{224,1... | collective-permute-start | bytes 393224 | tf_op jit(solution)/shard_map/ppermute | solution.py:495
  47.0 5.9 %collective-permute-start.1 = (f32[128,256]{1,0:T(8,128)S(1)}, f32[128,256]{1,0:T(8,128)S(1)}, u32[]{:S(2)}, u32[]{:S(2)}) collective-permute-start(f32[128,256]{1,0:T(8,128)S(1)} %get-tuple-element.28.pair_ref), channel_id=1, source_target_pairs={{0,64},{32,224},{64,128},{96,32},{128,192},{160,96},{192,0},{224,1... | collective-permute-start | bytes 393224 | tf_op jit(solution)/shard_map/ppermute | solution.py:495
  49.5 5.6 %collective-permute-start.3 = (f32[64,256]{1,0:T(8,128)S(1)}, f32[64,256]{1,0:T(8,128)S(1)}, u32[]{:S(2)}, u32[]{:S(2)}) collective-permute-start(f32[64,256]{1,0:T(8,128)S(1)} %get-tuple-element.29), channel_id=1, source_target_pairs={{0,128},{32,160},{64,192},{96,224},{128,0},{160,32},{192,64},{224,... | collective-permute-start | bytes 196616 | tf_op jit(solution)/shard_map/ppermute | solution.py:495
  52.8 4.0 %collective-permute-start.2 = (f32[128,256]{1,0:T(8,128)S(1)}, f32[128,256]{1,0:T(8,128)S(1)}, u32[]{:S(2)}, u32[]{:S(2)}) collective-permute-start(f32[128,256]{1,0:T(8,128)S(1)} %collective-permute-done.1.near_ref), channel_id=1, source_target_pairs={{0,32},{32,0},{64,96},{96,64},{128,160},{160,128},{192,224},{224,1... | collective-permute-start | bytes 393224 | tf_op jit(solution)/shard_map/ppermute | solution.py:495
  55.1 1.7 %collective-permute-start.4 = (f32[64,256]{1,0:T(8,128)S(1)}, f32[64,256]{1,0:T(8,128)S(1)}, u32[]{:S(2)}, u32[]{:S(2)}) collective-permute-start(f32[64,256]{1,0:T(8,128)S(1)} %collective-permute-done.3.far_ref), channel_id=1, source_target_pairs={{0,32},{32,0},{64,96},{96,64},{128,160},{160,128},{192,224},{224,1... | collective-permute-start | bytes 196616 | tf_op jit(solution)/shard_map/ppermute | solution.py:495

commit v3 on v1

--- a/solution.py
+++ b/solution.py
@@ -242,20 +242,16 @@
         copy.wait()
 
 
-def filter_kernel(in_ref, kernel_ref, rows_ref, out_ref, spec_ref, energy_ref, by_depth_ref):
+def filter_kernel(in_ref, kernel_ref, rows_ref, out_ref, spec_ref):
     slabs, _, lanes = in_ref.shape
     spec = spectrum(in_ref, rows_ref)
     cols = lanes // 8
-    weight = 0.0
     filtered = []
     for at, (real, imag) in enumerate(spec):
         spec_ref[2 * at * cols : (2 * at + 1) * cols] = real
         spec_ref[(2 * at + 1) * cols : (2 * at + 2) * cols] = imag
         kernel = at_depth(kernel_ref, at)
-        by_depth_ref[at * cols : (at + 1) * cols] = kernel
         filtered.append((kernel * real, kernel * imag))
-        weight = weight + (filtered[-1][0] * real + filtered[-1][1] * imag)
-    energy_ref[...] = jnp.broadcast_to(total(weight), energy_ref.shape)
     planes = shallow(filtered)
     real, imag = [jnp.concatenate([plane[part] for plane in planes], axis=0) for part in range(2)]
     high, low = pair_of(rows_ref, 0)
@@ -265,6 +261,20 @@
         rows = slice(at * length, (at + 1) * length)
         back = product((high[rows], low[rows]), split(jnp.concatenate(folded, axis=1)), NT)
         out_ref[:, at * 8 : (at + 1) * 8, :] = back.reshape(slabs, 8, lanes)
+
+
+def weigh_kernel(spec_ref, kernel_ref, vec_ref, _, norms_ref, by_depth_ref):
+    cols = spec_ref.shape[0] // 32
+    weight = 0.0
+    for at in range(16):
+        real, imag = spec_ref[2 * at * cols : (2 * at + 1) * cols], spec_ref[(2 * at + 1) * cols : (2 * at + 2) * cols]
+        kernel = at_depth(kernel_ref, at)
+        by_depth_ref[at * cols : (at + 1) * cols] = kernel
+        weight = weight + kernel * (real * real + imag * imag)
+    vec = vec_ref[...]
+    lanes = norms_ref.shape[1]
+    first = lax.broadcasted_iota(jnp.int32, norms_ref.shape, 0) == 0
+    norms_ref[...] = jnp.where(first, row_of(total(weight), lanes), row_of(total(vec * vec), lanes))
 
 
 def image_kernel(in_ref, sens_ref, table_ref, out_ref, straight_ref, turned_ref):
@@ -321,12 +331,12 @@
     out_ref[cells:] = sens_re * img_im - sens_im * img_re
 
 
-def add_kernel(own_ref, next_ref, last_ref, across_ref, out_ref):
+def add_kernel(own_ref, across_ref, last_ref, next_ref, _, out_ref):
     out_ref[...] = (own_ref[...] + across_ref[...]) + (next_ref[...] + last_ref[...])
 
 
 def turn_kernel(
-    lam_ref, one_ref, other_ref, vec_ref, sens_ref, table_ref, out_ref, image_ref, sums_ref, straight_ref, turned_ref
+    lam_ref, one_ref, other_ref, vec_ref, norms_ref, sens_ref, table_ref, out_ref, image_ref, sums_ref, straight_ref, turned_ref
 ):
     cells2, width = vec_ref.shape
     cells = cells2 // 2
@@ -335,7 +345,7 @@
     image_ref[...] = image
     real, imag = coil_product(sens_ref, image[:cells], image[cells:])
     send_columns(real, imag, pair_of(table_ref, 0).__getitem__, out_ref, straight_ref, turned_ref)
-    norm = total(vec * vec)
+    norm = norms_ref[1:2, 0:1]
     ratio = along(total(vec * image), norm)
     rest = image - ratio * vec
     row = lax.broadcasted_iota(jnp.int32, sums_ref.shape, 0)
@@ -449,10 +459,11 @@
         start_kernel, [block, *loaded], "hhhhh", [dma((len(sources) + filt.shape[1] // 128,)), *spaces]
     )(*sources)
     got = to_slabs(sent)
-    shapes = [block, (4 * lanes, 2 * width), (8, 128), (2 * lanes, 2 * width)]
-    back, before, energy_now, filt = call(filter_kernel, shapes, "vvv", (), 32)(got, filt, row_table)
+    back, before = call(filter_kernel, [block, (4 * lanes, 2 * width)], "vvv", (), 32)(got, filt, row_table)
     home = to_slabs(back)
     term = call(image_kernel, [(cells2, width)], "vvv", spaces)(home, sens, table)
+
+    norms, filt = call(weigh_kernel, [(8, 128), (2 * lanes, 2 * width)], "vvvv")(before, filt, vec, term)
 
     chips = coils // 2
 
@@ -462,14 +473,14 @@
         ]
         return lax.ppermute(term, "coil", pairs)
 
-    pair = call(add_kernel, [term.shape], "vvvv")(term, *[from_chip(shift) for shift in (1, 3, 2)])
+    pair = call(add_kernel, [term.shape], "vvvvv")(term, *[from_chip(shift) for shift in (2, 3, 1)], norms)
     other = lax.ppermute(pair, "coil", [(at, at ^ 1) for at in range(coils)])
-    sent, image, sums = call(turn_kernel, [block, (cells2, width), (8, 128)], "svvvvv", spaces)(
-        reg_weight, pair, other, vec, sens, table
+    sent, image, sums = call(turn_kernel, [block, (cells2, width), (8, 128)], "svvvvvv", spaces)(
+        reg_weight, pair, other, vec, norms, sens, table
     )
     got = to_slabs(sent)
     own = call(last_kernel, [(coils * slabs, 128)], "vvvvvv", (), 32)(
-        got, before, energy_now, sums, filt, row_table
+        got, before, norms, sums, filt, row_table
     )
     every = lax.all_to_all(own, ("coil", "slab"), 0, 0, tiled=True)
     result = call(solution_kernel, [(cells2, width)], "svvv")(reg_weight, every, vec, image)

time: 94.4 us -> 94.2 us (level)
    pallas_call x3 -> x4, Pallas kernels: 2.12 us -> 2.33 us  [the longest x1 1.39 us: shards(): call(filter_kernel, [block, (4 * lanes, 2 * width)], 'vvv', (), 32)]
where the time goes in v3:
time: 94.2 us; the launch traced here: 94 us
  blocking collectives  72.7 us (77%)
  starting transfers between devices  9.83 us (10%)
  Pallas kernels  6.97 us (7%)
  waiting for transfers between devices  3.82 us (4%)
    all_to_all x2, blocking collectives, shards(): got = to_slabs(sent)  37.7 us
    all_to_all x1, blocking collectives, shards(): every = lax.all_to_all(own, ('coil', 'slab'), 0, 0, tiled=True)  20 us
    all_to_all x1, blocking collectives, shards(): home = to_slabs(back)  15 us
    ppermute x1, starting transfers between devices, shards(): other = lax.ppermute(pair, 'coil', [(at, at ^ 1) for at in range(coils)])  5.54 us
    ppermute x3, starting transfers between devices, from_chip(): return lax.ppermute(term, 'coil', pairs)  4.29 us
    ppermute x3, waiting for transfers between devices, from_chip(): return lax.ppermute(term, 'coil', pairs)  3.48 us
    pallas_call x1, Pallas kernels, shards(): call(start_kernel, [block, *loaded], 'hhhhh', [dma((len(sources) + filt.s...  1.93 us
  transfers between devices with their start and end apart: 4, of which 3 were waited for; matrix products, arithmetic and copies ran while one was open for 0% of the time, Pallas kernels for 0%

profile of v3, /device:TPU:1, one launch (start us, length us, event | category | flops | bytes accessed | tf_op | source)
XLA Modules:
  0.0 94.0 jit_solution(4512926660242134016)
XLA Ops:
  0.0 1.9 %shard_map.64 = (f32[32,16,128]{2,1,0:T(8,128)S(1)}, f32[128,256]{1,0:T(8,128)S(1)}, f32[128,256]{1,0:T(8,128)S(1)}, bf16[1024,512]{1,0:T(8,128)(2,1)S(1)}, f32[...) custom-call(f32[128,256]{1,0:T(8,128)} %bitcast.11, f32[128,256]{1,0:T(8,128)} %bitcast.12, ...), custom_call_target="tpu_custom_call" | custom-call | tf_op jit(solution)/shard_map/pallas_call | solution.py:458
  1.9 23.0 %all_to_all.26.in_ref = f32[32,16,128]{2,1,0:T(8,128)S(1)} all-to-all(f32[32,16,128]{2,1,0:T(8,128)S(1)} %get-tuple-element.18), channel_id=1, replica_groups=mesh['coil'=8,'slab'=32] {'slab'}, dimensions={0} | all-to-all | bytes 524288 | tf_op jit(solution)/shard_map/all_to_all | solution.py:461
  25.0 1.4 %shard_map.65 = (f32[32,16,128]{2,1,0:T(8,128)S(1)}, f32[512,512]{1,0:T(8,128)S(1)}) custom-call(f32[32,16,128]{2,1,0:T(8,128)S(1)} %all_to_all.26.in_ref, f32[1024,128]{1,0:T(8,128)S(1)} %get-tuple-element.19.kernel_ref, bf16[1024,512]{1,0:T(8,128)(2,1)S(1)} %get-tuple-element.20.rows_ref), custom_call_target="tpu_custom_call" | custom-call | tf_op jit(solution)/shard_map/pallas_call | solution.py:462
  26.4 15.0 %all_to_all.27.in_ref = f32[32,16,128]{2,1,0:T(8,128)S(1)} all-to-all(f32[32,16,128]{2,1,0:T(8,128)S(1)} %get-tuple-element.21), channel_id=1, replica_groups=mesh['coil'=8,'slab'=32] {'slab'}, dimensions={0} | all-to-all | bytes 524288 | tf_op jit(solution)/shard_map/all_to_all | solution.py:463
  41.3 0.6 shard_map.66._.own_ref
  41.9 1.3 %collective-permute-start.2 = (f32[128,256]{1,0:T(8,128)S(1)}, f32[128,256]{1,0:T(8,128)S(1)}, u32[]{:S(2)}, u32[]{:S(2)}) collective-permute-start(f32[128,256]{1,0:T(8,128)S(1)} %shard_map.66._.own_ref), channel_id=1, source_target_pairs={{0,64},{32,96},{64,128},{96,160},{128,192},{160,224},{192,0},{224,... | collective-permute-start | bytes 393224 | tf_op jit(solution)/shard_map/ppermute | solution.py:474
  43.2 1.5 %collective-permute-start.1 = (f32[128,256]{1,0:T(8,128)S(1)}, f32[128,256]{1,0:T(8,128)S(1)}, u32[]{:S(2)}, u32[]{:S(2)}) collective-permute-start(f32[128,256]{1,0:T(8,128)S(1)} %shard_map.66._.own_ref), channel_id=1, source_target_pairs={{0,192},{32,224},{64,0},{96,32},{128,64},{160,96},{192,128},{224,1... | collective-permute-start | bytes 393224 | tf_op jit(solution)/shard_map/ppermute | solution.py:474
  44.7 1.5 %collective-permute-start = (f32[128,256]{1,0:T(8,128)S(1)}, f32[128,256]{1,0:T(8,128)S(1)}, u32[]{:S(2)}, u32[]{:S(2)}) collective-permute-start(f32[128,256]{1,0:T(8,128)S(1)} %shard_map.66._.own_ref), channel_id=1, source_target_pairs={{0,128},{32,160},{64,192},{96,224},{128,0},{160,32},{192,64},{224,... | collective-permute-start | bytes 393224 | tf_op jit(solution)/shard_map/ppermute | solution.py:474
  46.2 0.3 shard_map.67
  46.5 0.5 collective-permute-done.2.next_ref
  47.0 0.0 collective-permute-done.1.last_ref
  47.0 3.0 %collective-permute-done.across_ref = f32[128,256]{1,0:T(8,128)S(1)} collective-permute-done((f32[128,256]{1,0:T(8,128)S(1)}, f32[128,256]{1,0:T(8,128)S(1)}, u32[]{:S(2)}, u32[]{:S(2)}) %collective-permute-start) | collective-permute-done | bytes 131104 | tf_op jit(solution)/shard_map/ppermute | solution.py:474
  50.1 5.5 %collective-permute-start.3 = (f32[128,256]{1,0:T(8,128)S(1)}, f32[128,256]{1,0:T(8,128)S(1)}, u32[]{:S(2)}, u32[]{:S(2)}) collective-permute-start(f32[128,256]{1,0:T(8,128)S(1)} %shard_map.68.one_ref), channel_id=1, source_target_pairs={{0,32},{32,0},{64,96},{96,64},{128,160},{160,128},{192,224},{224,1... | collective-permute-start | bytes 393224 | tf_op jit(solution)/shard_map/ppermute | solution.py:477
  56.2 0.3 collective-permute-done.3.other_ref
  56.6 0.6 shard_map.69
  57.2 14.7 %all_to_all.28.in_ref = f32[32,16,128]{2,1,0:T(8,128)S(1)} all-to-all(f32[32,16,128]{2,1,0:T(8,128)S(1)} %get-tuple-element.27), channel_id=1, replica_groups=mesh['coil'=8,'slab'=32] {'slab'}, dimensions={0} | all-to-all | bytes 524288 | tf_op jit(solution)/shard_map/all_to_all | solution.py:481
  71.9 1.1 %shard_map.70 = f32[256,128]{1,0:T(8,128)S(1)} custom-call(f32[32,16,128]{2,1,0:T(8,128)S(1)} %all_to_all.28.in_ref, f32[512,512]{1,0:T(8,128)S(1)} %get-tuple-element.24.spec_ref.before_ref, f32[8,128]{1,0:T(8,128)S(1)} %get-tuple-element.26._.norms_ref.energy_ref, f32[8,128]{1,0:T(8,128)S(1)} %get-tuple-element.28.sums_ref, ...), custom_call_target="tpu_custom_call" | custom-call | tf_op jit(solution)/shard_map/pallas_call | solution.py:482
  73.0 20.0 %all_to_all.29 = f32[256,1,128]{2,1,0:T(1,128)S(1)} all-to-all(f32[256,1,128]{2,1,0:T(1,128)S(1)} %bitcast.8), channel_id=1, replica_groups=mesh['coil'=8,'slab'=32] {'coil','slab'}, dimensions={0} | all-to-all | bytes 262144 | tf_op jit(solution)/shard_map/all_to_all | solution.py:485
  93.0 1.0 %shard_map.71 = f32[128,256]{1,0:T(8,128)} custom-call(f32[1]{0:T(128)S(6)} %copy.8.lam_ref, f32[256,128]{1,0:T(8,128)S(1)} %bitcast.9, f32[128,256]{1,0:T(8,128)S(1)} %get-tuple-element.25.vec_ref, f32[128,256]{1,0:T(8,128)S(1)} %get-tuple-element.30.image_ref), custom_call_target="tpu_custom_call" | custom-call | tf_op jit(solution)/shard_map/pallas_call | solution.py:486
  (1 shorter events, 0.0 us)
Async XLA Ops:
  41.9 5.1 %collective-permute-start.2 = (f32[128,256]{1,0:T(8,128)S(1)}, f32[128,256]{1,0:T(8,128)S(1)}, u32[]{:S(2)}, u32[]{:S(2)}) collective-permute-start(f32[128,256]{1,0:T(8,128)S(1)} %shard_map.66._.own_ref), channel_id=1, source_target_pairs={{0,64},{32,96},{64,128},{96,160},{128,192},{160,224},{192,0},{224,... | collective-permute-start | bytes 393224 | tf_op jit(solution)/shard_map/ppermute | solution.py:474
  43.2 3.8 %collective-permute-start.1 = (f32[128,256]{1,0:T(8,128)S(1)}, f32[128,256]{1,0:T(8,128)S(1)}, u32[]{:S(2)}, u32[]{:S(2)}) collective-permute-start(f32[128,256]{1,0:T(8,128)S(1)} %shard_map.66._.own_ref), channel_id=1, source_target_pairs={{0,192},{32,224},{64,0},{96,32},{128,64},{160,96},{192,128},{224,1... | collective-permute-start | bytes 393224 | tf_op jit(solution)/shard_map/ppermute | solution.py:474
  44.7 5.3 %collective-permute-start = (f32[128,256]{1,0:T(8,128)S(1)}, f32[128,256]{1,0:T(8,128)S(1)}, u32[]{:S(2)}, u32[]{:S(2)}) collective-permute-start(f32[128,256]{1,0:T(8,128)S(1)} %shard_map.66._.own_ref), channel_id=1, source_target_pairs={{0,128},{32,160},{64,192},{96,224},{128,0},{160,32},{192,64},{224,... | collective-permute-start | bytes 393224 | tf_op jit(solution)/shard_map/ppermute | solution.py:474
  50.1 6.5 %collective-permute-start.3 = (f32[128,256]{1,0:T(8,128)S(1)}, f32[128,256]{1,0:T(8,128)S(1)}, u32[]{:S(2)}, u32[]{:S(2)}) collective-permute-start(f32[128,256]{1,0:T(8,128)S(1)} %shard_map.68.one_ref), channel_id=1, source_target_pairs={{0,32},{32,0},{64,96},{96,64},{128,160},{160,128},{192,224},{224,1... | collective-permute-start | bytes 393224 | tf_op jit(solution)/shard_map/ppermute | solution.py:477

commit v4 on v3

--- a/solution.py
+++ b/solution.py
@@ -263,14 +263,17 @@
         out_ref[:, at * 8 : (at + 1) * 8, :] = back.reshape(slabs, 8, lanes)
 
 
-def weigh_kernel(spec_ref, kernel_ref, vec_ref, _, norms_ref, by_depth_ref):
+def weigh_kernel(spec_ref, kernel_ref, vec_ref, _, norms_ref, by_depth_ref, weighted_ref):
     cols = spec_ref.shape[0] // 32
     weight = 0.0
     for at in range(16):
         real, imag = spec_ref[2 * at * cols : (2 * at + 1) * cols], spec_ref[(2 * at + 1) * cols : (2 * at + 2) * cols]
         kernel = at_depth(kernel_ref, at)
         by_depth_ref[at * cols : (at + 1) * cols] = kernel
-        weight = weight + kernel * (real * real + imag * imag)
+        heavy, heavy_imag = kernel * real, kernel * imag
+        weighted_ref[2 * at * cols : (2 * at + 1) * cols] = heavy
+        weighted_ref[(2 * at + 1) * cols : (2 * at + 2) * cols] = heavy_imag
+        weight = weight + (heavy * real + heavy_imag * imag)
     vec = vec_ref[...]
     lanes = norms_ref.shape[1]
     first = lax.broadcasted_iota(jnp.int32, norms_ref.shape, 0) == 0
@@ -357,25 +360,25 @@
     )
 
 
-def last_kernel(in_ref, before_ref, energy_ref, sums_ref, by_depth_ref, rows_ref, out_ref):
+def last_kernel(in_ref, before_ref, weighted_ref, energy_ref, sums_ref, by_depth_ref, rows_ref, out_ref):
     spec = spectrum(in_ref, rows_ref)
     cols = spec[0][0].shape[0]
     norm = energy_ref[0:1, 0:1]
 
-    def before(at):
-        return before_ref[2 * at * cols : (2 * at + 1) * cols], before_ref[(2 * at + 1) * cols : (2 * at + 2) * cols]
+    def of(ref, at):
+        return ref[2 * at * cols : (2 * at + 1) * cols], ref[(2 * at + 1) * cols : (2 * at + 2) * cols]
 
     def kernel(at):
         return by_depth_ref[at * cols : (at + 1) * cols]
 
     weight = 0.0
     for at, (real, imag) in enumerate(spec):
-        real_0, imag_0 = before(at)
-        weight = weight + kernel(at) * (real * real_0 + imag * imag_0)
+        real_0, imag_0 = of(weighted_ref, at)
+        weight = weight + (real * real_0 + imag * imag_0)
     ratio = along(total(weight), norm)
     weight = 0.0
     for at, (real, imag) in enumerate(spec):
-        real_0, imag_0 = before(at)
+        real_0, imag_0 = of(before_ref, at)
         real, imag = real - ratio * real_0, imag - ratio * imag_0
         weight = weight + kernel(at) * (real * real + imag * imag)
     lanes = out_ref.shape[1]
@@ -463,7 +466,8 @@
     home = to_slabs(back)
     term = call(image_kernel, [(cells2, width)], "vvv", spaces)(home, sens, table)
 
-    norms, filt = call(weigh_kernel, [(8, 128), (2 * lanes, 2 * width)], "vvvv")(before, filt, vec, term)
+    shapes = [(8, 128), (2 * lanes, 2 * width), (4 * lanes, 2 * width)]
+    norms, filt, weighted = call(weigh_kernel, shapes, "vvvv")(before, filt, vec, term)
 
     chips = coils // 2
 
@@ -479,8 +483,8 @@
         reg_weight, pair, other, vec, norms, sens, table
     )
     got = to_slabs(sent)
-    own = call(last_kernel, [(coils * slabs, 128)], "vvvvvv", (), 32)(
-        got, before, norms, sums, filt, row_table
+    own = call(last_kernel, [(coils * slabs, 128)], "vvvvvvv", (), 32)(
+        got, before, weighted, norms, sums, filt, row_table
     )
     every = lax.all_to_all(own, ("coil", "slab"), 0, 0, tiled=True)
     result = call(solution_kernel, [(cells2, width)], "svvv")(reg_weight, every, vec, image)

time: 94.2 us -> 94.6 us (level)
  waiting for transfers between devices: 3.82 us -> 5.75 us
  starting transfers between devices: 9.83 us -> 8.44 us
    ppermute x3, waiting for transfers between devices: 3.48 us -> 5.41 us  [from_chip(): return lax.ppermute(term, 'coil', pairs)]
    ppermute x1, starting transfers between devices: 5.54 us -> 4.14 us  [shards(): other = lax.ppermute(pair, 'coil', [(at, at ^ 1) for at in range(coils)])]
  transfers between devices with their start and end apart: 4 -> 4, of which waited for: 3 -> 4; matrix products, arithmetic and copies ran while one was open for 0% -> 0% of each run, Pallas kernels for 0% -> 0%
where the time goes in v4:
time: 94.6 us; the launch traced here: 94.3 us
  blocking collectives  72.4 us (77%)
  starting transfers between devices  8.44 us (9%)
  Pallas kernels  7.01 us (7%)
  waiting for transfers between devices  5.75 us (6%)
    all_to_all x2, blocking collectives, shards(): got = to_slabs(sent)  37.7 us
    all_to_all x1, blocking collectives, shards(): every = lax.all_to_all(own, ('coil', 'slab'), 0, 0, tiled=True)  19.7 us
    all_to_all x1, blocking collectives, shards(): home = to_slabs(back)  15 us
    ppermute x3, waiting for transfers between devices, from_chip(): return lax.ppermute(term, 'coil', pairs)  5.41 us
    ppermute x3, starting transfers between devices, from_chip(): return lax.ppermute(term, 'coil', pairs)  4.3 us
    ppermute x1, starting transfers between devices, shards(): other = lax.ppermute(pair, 'coil', [(at, at ^ 1) for at in range(coils)])  4.14 us
    pallas_call x1, Pallas kernels, shards(): call(start_kernel, [block, *loaded], 'hhhhh', [dma((len(sources) + filt.s...  1.93 us
  transfers between devices with their start and end apart: 4, of which 4 were waited for; matrix products, arithmetic and copies ran while one was open for 0% of the time, Pallas kernels for 0%

profile of v4, /device:TPU:1, one launch (start us, length us, event | category | flops | bytes accessed | tf_op | source)
XLA Modules:
  0.0 94.3 jit_solution(9896702862383080661)
XLA Ops:
  0.0 1.9 %shard_map.64 = (f32[32,16,128]{2,1,0:T(8,128)S(1)}, f32[128,256]{1,0:T(8,128)S(1)}, f32[128,256]{1,0:T(8,128)S(1)}, bf16[1024,512]{1,0:T(8,128)(2,1)S(1)}, f32[...) custom-call(f32[128,256]{1,0:T(8,128)} %bitcast.11, f32[128,256]{1,0:T(8,128)} %bitcast.12, ...), custom_call_target="tpu_custom_call" | custom-call | tf_op jit(solution)/shard_map/pallas_call | solution.py:461
  1.9 23.0 %all_to_all.26.in_ref = f32[32,16,128]{2,1,0:T(8,128)S(1)} all-to-all(f32[32,16,128]{2,1,0:T(8,128)S(1)} %get-tuple-element.19), channel_id=1, replica_groups=mesh['coil'=8,'slab'=32] {'slab'}, dimensions={0} | all-to-all | bytes 524288 | tf_op jit(solution)/shard_map/all_to_all | solution.py:464
  25.0 1.4 %shard_map.65 = (f32[32,16,128]{2,1,0:T(8,128)S(1)}, f32[512,512]{1,0:T(8,128)S(1)}) custom-call(f32[32,16,128]{2,1,0:T(8,128)S(1)} %all_to_all.26.in_ref, f32[1024,128]{1,0:T(8,128)S(1)} %get-tuple-element.20.kernel_ref, bf16[1024,512]{1,0:T(8,128)(2,1)S(1)} %get-tuple-element.21.rows_ref), custom_call_target="tpu_custom_call" | custom-call | tf_op jit(solution)/shard_map/pallas_call | solution.py:465
  26.4 15.0 %all_to_all.27.in_ref = f32[32,16,128]{2,1,0:T(8,128)S(1)} all-to-all(f32[32,16,128]{2,1,0:T(8,128)S(1)} %get-tuple-element.22), channel_id=1, replica_groups=mesh['coil'=8,'slab'=32] {'slab'}, dimensions={0} | all-to-all | bytes 524288 | tf_op jit(solution)/shard_map/all_to_all | solution.py:466
  41.3 0.6 shard_map.66._.own_ref
  41.9 2.8 %collective-permute-start = (f32[128,256]{1,0:T(8,128)S(1)}, f32[128,256]{1,0:T(8,128)S(1)}, u32[]{:S(2)}, u32[]{:S(2)}) collective-permute-start(f32[128,256]{1,0:T(8,128)S(1)} %shard_map.66._.own_ref), channel_id=1, source_target_pairs={{0,128},{32,160},{64,192},{96,224},{128,0},{160,32},{192,64},{224,... | collective-permute-start | bytes 393224 | tf_op jit(solution)/shard_map/ppermute | solution.py:478
  44.8 0.9 collective-permute-start.1
  45.6 0.6 collective-permute-start.2
  46.2 0.4 shard_map.67
  46.6 0.7 collective-permute-done.across_ref
  47.3 1.5 %collective-permute-done.1.last_ref = f32[128,256]{1,0:T(8,128)S(1)} collective-permute-done((f32[128,256]{1,0:T(8,128)S(1)}, f32[128,256]{1,0:T(8,128)S(1)}, u32[]{:S(2)}, u32[]{:S(2)}) %collective-permute-start.1) | collective-permute-done | bytes 131104 | tf_op jit(solution)/shard_map/ppermute | solution.py:478
  48.8 3.2 %collective-permute-done.2.next_ref = f32[128,256]{1,0:T(8,128)S(1)} collective-permute-done((f32[128,256]{1,0:T(8,128)S(1)}, f32[128,256]{1,0:T(8,128)S(1)}, u32[]{:S(2)}, u32[]{:S(2)}) %collective-permute-start.2) | collective-permute-done | bytes 131104 | tf_op jit(solution)/shard_map/ppermute | solution.py:478
  52.1 4.1 %collective-permute-start.3 = (f32[128,256]{1,0:T(8,128)S(1)}, f32[128,256]{1,0:T(8,128)S(1)}, u32[]{:S(2)}, u32[]{:S(2)}) collective-permute-start(f32[128,256]{1,0:T(8,128)S(1)} %shard_map.68.one_ref), channel_id=1, source_target_pairs={{0,32},{32,0},{64,96},{96,64},{128,160},{160,128},{192,224},{224,1... | collective-permute-start | bytes 393224 | tf_op jit(solution)/shard_map/ppermute | solution.py:481
  56.9 0.3 collective-permute-done.3.other_ref
  57.2 0.6 shard_map.69
  57.8 14.7 %all_to_all.28.in_ref = f32[32,16,128]{2,1,0:T(8,128)S(1)} all-to-all(f32[32,16,128]{2,1,0:T(8,128)S(1)} %get-tuple-element.28), channel_id=1, replica_groups=mesh['coil'=8,'slab'=32] {'slab'}, dimensions={0} | all-to-all | bytes 524288 | tf_op jit(solution)/shard_map/all_to_all | solution.py:485
  72.5 1.1 %shard_map.70 = f32[256,128]{1,0:T(8,128)S(1)} custom-call(f32[32,16,128]{2,1,0:T(8,128)S(1)} %all_to_all.28.in_ref, f32[512,512]{1,0:T(8,128)S(1)} %get-tuple-element.25.spec_ref.before_ref, f32[512,512]{1,0:T(8,128)S(1)} %get-tuple-element.29.weighted_ref, f32[8,128]{1,0:T(8,128)S(1)} %get-tuple-element.27._.norms_ref.energy_ref, ...), custom_call_target="tpu_custom_call" | custom-call | tf_op jit(solution)/shard_map/pallas_call | solution.py:486
  73.6 19.7 %all_to_all.29 = f32[256,1,128]{2,1,0:T(1,128)S(1)} all-to-all(f32[256,1,128]{2,1,0:T(1,128)S(1)} %bitcast.8), channel_id=1, replica_groups=mesh['coil'=8,'slab'=32] {'coil','slab'}, dimensions={0} | all-to-all | bytes 262144 | tf_op jit(solution)/shard_map/all_to_all | solution.py:489
  93.3 1.0 %shard_map.71 = f32[128,256]{1,0:T(8,128)} custom-call(f32[1]{0:T(128)S(6)} %copy.8.lam_ref, f32[256,128]{1,0:T(8,128)S(1)} %bitcast.9, f32[128,256]{1,0:T(8,128)S(1)} %get-tuple-element.26.vec_ref, f32[128,256]{1,0:T(8,128)S(1)} %get-tuple-element.32.image_ref), custom_call_target="tpu_custom_call" | custom-call | tf_op jit(solution)/shard_map/pallas_call | solution.py:490
  (1 shorter events, 0.0 us)
Async XLA Ops:
  41.9 5.4 %collective-permute-start = (f32[128,256]{1,0:T(8,128)S(1)}, f32[128,256]{1,0:T(8,128)S(1)}, u32[]{:S(2)}, u32[]{:S(2)}) collective-permute-start(f32[128,256]{1,0:T(8,128)S(1)} %shard_map.66._.own_ref), channel_id=1, source_target_pairs={{0,128},{32,160},{64,192},{96,224},{128,0},{160,32},{192,64},{224,... | collective-permute-start | bytes 393224 | tf_op jit(solution)/shard_map/ppermute | solution.py:478
  44.8 4.1 %collective-permute-start.1 = (f32[128,256]{1,0:T(8,128)S(1)}, f32[128,256]{1,0:T(8,128)S(1)}, u32[]{:S(2)}, u32[]{:S(2)}) collective-permute-start(f32[128,256]{1,0:T(8,128)S(1)} %shard_map.66._.own_ref), channel_id=1, source_target_pairs={{0,192},{32,224},{64,0},{96,32},{128,64},{160,96},{192,128},{224,1... | collective-permute-start | bytes 393224 | tf_op jit(solution)/shard_map/ppermute | solution.py:478
  45.6 6.4 %collective-permute-start.2 = (f32[128,256]{1,0:T(8,128)S(1)}, f32[128,256]{1,0:T(8,128)S(1)}, u32[]{:S(2)}, u32[]{:S(2)}) collective-permute-start(f32[128,256]{1,0:T(8,128)S(1)} %shard_map.66._.own_ref), channel_id=1, source_target_pairs={{0,64},{32,96},{64,128},{96,160},{128,192},{160,224},{192,0},{224,... | collective-permute-start | bytes 393224 | tf_op jit(solution)/shard_map/ppermute | solution.py:478
  52.1 5.1 %collective-permute-start.3 = (f32[128,256]{1,0:T(8,128)S(1)}, f32[128,256]{1,0:T(8,128)S(1)}, u32[]{:S(2)}, u32[]{:S(2)}) collective-permute-start(f32[128,256]{1,0:T(8,128)S(1)} %shard_map.68.one_ref), channel_id=1, source_target_pairs={{0,32},{32,0},{64,96},{96,64},{128,160},{160,128},{192,224},{224,1... | collective-permute-start | bytes 393224 | tf_op jit(solution)/shard_map/ppermute | solution.py:481

commit v5 on v4

--- a/solution.py
+++ b/solution.py
@@ -334,7 +334,7 @@
     out_ref[cells:] = sens_re * img_im - sens_im * img_re
 
 
-def add_kernel(own_ref, across_ref, last_ref, next_ref, _, out_ref):
+def add_kernel(own_ref, across_ref, next_ref, last_ref, _, out_ref):
     out_ref[...] = (own_ref[...] + across_ref[...]) + (next_ref[...] + last_ref[...])
 
 
@@ -477,7 +477,7 @@
         ]
         return lax.ppermute(term, "coil", pairs)
 
-    pair = call(add_kernel, [term.shape], "vvvvv")(term, *[from_chip(shift) for shift in (2, 3, 1)], norms)
+    pair = call(add_kernel, [term.shape], "vvvvv")(term, *[from_chip(shift) for shift in (2, 1, 3)], norms)
     other = lax.ppermute(pair, "coil", [(at, at ^ 1) for at in range(coils)])
     sent, image, sums = call(turn_kernel, [block, (cells2, width), (8, 128)], "svvvvvv", spaces)(
         reg_weight, pair, other, vec, norms, sens, table

time: 94.6 us -> 95.1 us (level)
  waiting for transfers between devices: 5.75 us -> 2.28 us
  starting transfers between devices: 8.44 us -> 10.8 us
  blocking collectives: 72.4 us -> 74.1 us
    ppermute x3, waiting for transfers between devices: 5.41 us -> 1.95 us  [from_chip(): return lax.ppermute(term, 'coil', pairs)]
    all_to_all x1, blocking collectives: 19.7 us -> 21.4 us  [shards(): every = lax.all_to_all(own, ('coil', 'slab'), 0, 0, tiled=True)]
    ppermute x3, starting transfers between devices: 4.3 us -> 5.51 us  [from_chip(): return lax.ppermute(term, 'coil', pairs)]
    ppermute x1, starting transfers between devices: 4.14 us -> 5.27 us  [shards(): other = lax.ppermute(pair, 'coil', [(at, at ^ 1) for at in range(coils)])]
  transfers between devices with their start and end apart: 4 -> 4, of which waited for: 4 -> 2; matrix products, arithmetic and copies ran while one was open for 0% -> 0% of each run, Pallas kernels for 0% -> 0%
where the time goes in v5:
time: 95.1 us; the launch traced here: 94.9 us
  blocking collectives  74.1 us (78%)
  starting transfers between devices  10.8 us (11%)
  Pallas kernels  7.02 us (7%)
  waiting for transfers between devices  2.28 us (2%)
    all_to_all x2, blocking collectives, shards(): got = to_slabs(sent)  37.7 us
    all_to_all x1, blocking collectives, shards(): every = lax.all_to_all(own, ('coil', 'slab'), 0, 0, tiled=True)  21.4 us
    all_to_all x1, blocking collectives, shards(): home = to_slabs(back)  15 us
    ppermute x3, starting transfers between devices, from_chip(): return lax.ppermute(term, 'coil', pairs)  5.51 us
    ppermute x1, starting transfers between devices, shards(): other = lax.ppermute(pair, 'coil', [(at, at ^ 1) for at in range(coils)])  5.27 us
    ppermute x3, waiting for transfers between devices, from_chip(): return lax.ppermute(term, 'coil', pairs)  1.95 us
    pallas_call x1, Pallas kernels, shards(): call(start_kernel, [block, *loaded], 'hhhhh', [dma((len(sources) + filt.s...  1.93 us
  transfers between devices with their start and end apart: 4, of which 2 were waited for; matrix products, arithmetic and copies ran while one was open for 0% of the time, Pallas kernels for 0%

profile of v5, /device:TPU:1, one launch (start us, length us, event | category | flops | bytes accessed | tf_op | source)
XLA Modules:
  0.0 94.9 jit_solution(15610142877579012496)
XLA Ops:
  0.0 1.9 %shard_map.64 = (f32[32,16,128]{2,1,0:T(8,128)S(1)}, f32[128,256]{1,0:T(8,128)S(1)}, f32[128,256]{1,0:T(8,128)S(1)}, bf16[1024,512]{1,0:T(8,128)(2,1)S(1)}, f32[...) custom-call(f32[128,256]{1,0:T(8,128)} %bitcast.11, f32[128,256]{1,0:T(8,128)} %bitcast.12, ...), custom_call_target="tpu_custom_call" | custom-call | tf_op jit(solution)/shard_map/pallas_call | solution.py:461
  1.9 23.0 %all_to_all.26.in_ref = f32[32,16,128]{2,1,0:T(8,128)S(1)} all-to-all(f32[32,16,128]{2,1,0:T(8,128)S(1)} %get-tuple-element.19), channel_id=1, replica_groups=mesh['coil'=8,'slab'=32] {'slab'}, dimensions={0} | all-to-all | bytes 524288 | tf_op jit(solution)/shard_map/all_to_all | solution.py:464
  25.0 1.4 %shard_map.65 = (f32[32,16,128]{2,1,0:T(8,128)S(1)}, f32[512,512]{1,0:T(8,128)S(1)}) custom-call(f32[32,16,128]{2,1,0:T(8,128)S(1)} %all_to_all.26.in_ref, f32[1024,128]{1,0:T(8,128)S(1)} %get-tuple-element.20.kernel_ref, bf16[1024,512]{1,0:T(8,128)(2,1)S(1)} %get-tuple-element.21.rows_ref), custom_call_target="tpu_custom_call" | custom-call | tf_op jit(solution)/shard_map/pallas_call | solution.py:465
  26.4 15.0 %all_to_all.27.in_ref = f32[32,16,128]{2,1,0:T(8,128)S(1)} all-to-all(f32[32,16,128]{2,1,0:T(8,128)S(1)} %get-tuple-element.22), channel_id=1, replica_groups=mesh['coil'=8,'slab'=32] {'slab'}, dimensions={0} | all-to-all | bytes 524288 | tf_op jit(solution)/shard_map/all_to_all | solution.py:466
  41.3 0.6 shard_map.66._.own_ref
  41.9 2.8 %collective-permute-start = (f32[128,256]{1,0:T(8,128)S(1)}, f32[128,256]{1,0:T(8,128)S(1)}, u32[]{:S(2)}, u32[]{:S(2)}) collective-permute-start(f32[128,256]{1,0:T(8,128)S(1)} %shard_map.66._.own_ref), channel_id=1, source_target_pairs={{0,128},{32,160},{64,192},{96,224},{128,0},{160,32},{192,64},{224,... | collective-permute-start | bytes 393224 | tf_op jit(solution)/shard_map/ppermute | solution.py:478
  44.8 0.3 collective-permute-start.1
  45.1 2.4 %collective-permute-start.2 = (f32[128,256]{1,0:T(8,128)S(1)}, f32[128,256]{1,0:T(8,128)S(1)}, u32[]{:S(2)}, u32[]{:S(2)}) collective-permute-start(f32[128,256]{1,0:T(8,128)S(1)} %shard_map.66._.own_ref), channel_id=1, source_target_pairs={{0,192},{32,224},{64,0},{96,32},{128,64},{160,96},{192,128},{224,1... | collective-permute-start | bytes 393224 | tf_op jit(solution)/shard_map/ppermute | solution.py:478
  47.4 0.4 shard_map.67
  47.9 0.0 collective-permute-done.across_ref
  47.9 1.9 %collective-permute-done.1.next_ref = f32[128,256]{1,0:T(8,128)S(1)} collective-permute-done((f32[128,256]{1,0:T(8,128)S(1)}, f32[128,256]{1,0:T(8,128)S(1)}, u32[]{:S(2)}, u32[]{:S(2)}) %collective-permute-start.1) | collective-permute-done | bytes 131104 | tf_op jit(solution)/shard_map/ppermute | solution.py:478
  49.8 0.0 collective-permute-done.2.last_ref
  49.8 5.3 %collective-permute-start.3 = (f32[128,256]{1,0:T(8,128)S(1)}, f32[128,256]{1,0:T(8,128)S(1)}, u32[]{:S(2)}, u32[]{:S(2)}) collective-permute-start(f32[128,256]{1,0:T(8,128)S(1)} %shard_map.68.one_ref), channel_id=1, source_target_pairs={{0,32},{32,0},{64,96},{96,64},{128,160},{160,128},{192,224},{224,1... | collective-permute-start | bytes 393224 | tf_op jit(solution)/shard_map/ppermute | solution.py:481
  55.8 0.3 collective-permute-done.3.other_ref
  56.1 0.6 shard_map.69
  56.7 14.7 %all_to_all.28.in_ref = f32[32,16,128]{2,1,0:T(8,128)S(1)} all-to-all(f32[32,16,128]{2,1,0:T(8,128)S(1)} %get-tuple-element.28), channel_id=1, replica_groups=mesh['coil'=8,'slab'=32] {'slab'}, dimensions={0} | all-to-all | bytes 524288 | tf_op jit(solution)/shard_map/all_to_all | solution.py:485
  71.4 1.1 %shard_map.70 = f32[256,128]{1,0:T(8,128)S(1)} custom-call(f32[32,16,128]{2,1,0:T(8,128)S(1)} %all_to_all.28.in_ref, f32[512,512]{1,0:T(8,128)S(1)} %get-tuple-element.25.spec_ref.before_ref, f32[512,512]{1,0:T(8,128)S(1)} %get-tuple-element.29.weighted_ref, f32[8,128]{1,0:T(8,128)S(1)} %get-tuple-element.27._.norms_ref.energy_ref, ...), custom_call_target="tpu_custom_call" | custom-call | tf_op jit(solution)/shard_map/pallas_call | solution.py:486
  72.5 21.4 %all_to_all.29 = f32[256,1,128]{2,1,0:T(1,128)S(1)} all-to-all(f32[256,1,128]{2,1,0:T(1,128)S(1)} %bitcast.8), channel_id=1, replica_groups=mesh['coil'=8,'slab'=32] {'coil','slab'}, dimensions={0} | all-to-all | bytes 262144 | tf_op jit(solution)/shard_map/all_to_all | solution.py:489
  93.9 1.0 %shard_map.71 = f32[128,256]{1,0:T(8,128)} custom-call(f32[1]{0:T(128)S(6)} %copy.8.lam_ref, f32[256,128]{1,0:T(8,128)S(1)} %bitcast.9, f32[128,256]{1,0:T(8,128)S(1)} %get-tuple-element.26.vec_ref, f32[128,256]{1,0:T(8,128)S(1)} %get-tuple-element.32.image_ref), custom_call_target="tpu_custom_call" | custom-call | tf_op jit(solution)/shard_map/pallas_call | solution.py:490
  (1 shorter events, 0.0 us)
Async XLA Ops:
  41.9 5.9 %collective-permute-start = (f32[128,256]{1,0:T(8,128)S(1)}, f32[128,256]{1,0:T(8,128)S(1)}, u32[]{:S(2)}, u32[]{:S(2)}) collective-permute-start(f32[128,256]{1,0:T(8,128)S(1)} %shard_map.66._.own_ref), channel_id=1, source_target_pairs={{0,128},{32,160},{64,192},{96,224},{128,0},{160,32},{192,64},{224,... | collective-permute-start | bytes 393224 | tf_op jit(solution)/shard_map/ppermute | solution.py:478
  44.8 5.0 %collective-permute-start.1 = (f32[128,256]{1,0:T(8,128)S(1)}, f32[128,256]{1,0:T(8,128)S(1)}, u32[]{:S(2)}, u32[]{:S(2)}) collective-permute-start(f32[128,256]{1,0:T(8,128)S(1)} %shard_map.66._.own_ref), channel_id=1, source_target_pairs={{0,64},{32,96},{64,128},{96,160},{128,192},{160,224},{192,0},{224,... | collective-permute-start | bytes 393224 | tf_op jit(solution)/shard_map/ppermute | solution.py:478
  45.1 4.7 %collective-permute-start.2 = (f32[128,256]{1,0:T(8,128)S(1)}, f32[128,256]{1,0:T(8,128)S(1)}, u32[]{:S(2)}, u32[]{:S(2)}) collective-permute-start(f32[128,256]{1,0:T(8,128)S(1)} %shard_map.66._.own_ref), channel_id=1, source_target_pairs={{0,192},{32,224},{64,0},{96,32},{128,64},{160,96},{192,128},{224,1... | collective-permute-start | bytes 393224 | tf_op jit(solution)/shard_map/ppermute | solution.py:478
  49.8 6.3 %collective-permute-start.3 = (f32[128,256]{1,0:T(8,128)S(1)}, f32[128,256]{1,0:T(8,128)S(1)}, u32[]{:S(2)}, u32[]{:S(2)}) collective-permute-start(f32[128,256]{1,0:T(8,128)S(1)} %shard_map.68.one_ref), channel_id=1, source_target_pairs={{0,32},{32,0},{64,96},{96,64},{128,160},{160,128},{192,224},{224,1... | collective-permute-start | bytes 393224 | tf_op jit(solution)/shard_map/ppermute | solution.py:481
